TPU v7x, 512 devices: a whole 4x4x16 slice. The times are simulated.
512 devices in a mesh: half: 2 (over core), row: 16 (over z), col: 16 (over y, x).
Axes of the slice: x: 4, y: 4, z: 16, core: 2. Of those that a mesh axis runs over, the one named last changes fastest.
Arguments:
- child_front: float32 [2, 8192, 8192], P('half', 'row', 'col'), as said below
- child_map: int32 [2, 48], P('half'), may hold values from 0 to 63, as said below
- root_front: float32 [8192, 16, 2, 256], P('row', 'col', 'half'), as said below
Outputs:
- child_panel: float32 [2, 512, 8192], P('half', None, 'col')
- root_panel: float32 [512, 16, 2, 256], P(None, 'col', 'half')
- root_update: float32 [8192, 16, 2, 256], P('row', 'col', 'half')
Inputs may be any that keep to these rules, and one draw needn't show every extreme that they name: `child_map`: for child h, the update blocks of row part k (the 3 blocks after that part's first block) map in increasing order to distinct blocks among the root's blocks k * 4 to (k + 1) * 4 - 1. `child_front`: each child's front is symmetric and positive definite. `root_front`: the root front is symmetric and positive definite.
All inputs are finite; a program needn't handle non-finite values.
Results may differ from a plain program's by a relative error of at most 0.0001.
Values sent between devices are 32-bit elements; how exact they have to be, the bound alone decides.
A program may use at most 64 MiB of HBM per device.

v0:
```python
import jax
import jax.numpy as jnp
from jax import lax
from jax.sharding import PartitionSpec as P

BLK = 128
PB = 32


def spread_2(value, axis, source):
    kept = jnp.where(lax.axis_index(axis) == source, value, 0).astype(value.dtype)
    return lax.psum(kept, axis)


def lower_solve(factor, right):
    return lax.linalg.triangular_solve(factor, right, left_side=True, lower=True)


def transposed_product(left, right):
    return lax.dot_general(
        left,
        right,
        (((0,), (0,)), ((), ())),
        precision=lax.Precision.HIGHEST,
        preferred_element_type=jnp.float32,
    )


def selector(child_row_map, part_index, child_tiles, root_tiles):
    per_part = child_tiles - 1
    targets = (
        lax.dynamic_slice_in_dim(child_row_map, part_index * per_part, per_part)
        - part_index * root_tiles
    )
    one_hot = (jnp.arange(root_tiles, dtype=jnp.int32)[:, None] == targets[None, :]).astype(
        jnp.float32
    )
    return jnp.concatenate([jnp.zeros((root_tiles, 1), jnp.float32), one_hot], axis=1)


def body(child_front, child_map, root_front):
    tile_rows = BLK
    pivot_count = PB
    child_block = child_front[0]
    part_rows = child_block.shape[0]
    row_part = lax.axis_index("row")
    col_part = lax.axis_index("col")
    strips = lax.all_gather(child_block[:pivot_count, :], "row", axis=0, tiled=True)
    pieces = lax.all_gather(
        child_block[None, :pivot_count, :pivot_count], ("row", "col"), axis=0, tiled=True
    )
    parts_count = lax.axis_size("row")
    corner = pieces.reshape(parts_count, parts_count, pivot_count, pivot_count).transpose(
        0, 2, 1, 3
    )
    corner = corner.reshape(parts_count * pivot_count, parts_count * pivot_count)
    factor = jnp.linalg.cholesky(corner)
    child_panel = lower_solve(factor, strips)
    columns = lax.all_gather(child_block[:, :pivot_count], "col", axis=1, tiled=True)
    panel_rows = lower_solve(factor, columns.T)
    update = child_block - transposed_product(panel_rows, child_panel)
    root_rows = root_front.shape[0]
    child_tiles = part_rows // tile_rows
    root_tiles = root_rows // tile_rows
    own_map = child_map[0]
    row_select = selector(own_map, row_part, child_tiles, root_tiles)
    col_select = selector(own_map, col_part, child_tiles, root_tiles)
    blocks = update.reshape(child_tiles, tile_rows, child_tiles, tile_rows)
    spread = jnp.einsum("ap,piqj->aiqj", row_select, blocks, precision=lax.Precision.HIGHEST)
    spread = jnp.einsum("aiqj,bq->aibj", spread, col_select, precision=lax.Precision.HIGHEST)
    additions = spread.reshape(root_rows, 2, root_rows // 2)
    joined = lax.psum_scatter(additions, "half", scatter_dimension=1, tiled=True)
    assembled = root_front[:, 0, 0, :] + joined[:, 0, :]
    root_strips = lax.all_gather(assembled[:pivot_count, :], "row", axis=0, tiled=True)
    pivots = spread_2(root_strips[:, :pivot_count], "half", 0)
    root_corner = lax.all_gather(pivots, "col", axis=1, tiled=True)
    root_factor = jnp.linalg.cholesky(root_corner)
    root_panel = lower_solve(root_factor, root_strips)
    mirrored = spread_2(root_panel, "col", row_part)
    both_halves = lax.all_gather(mirrored[:, None, :], "half", axis=1, tiled=True)
    panel_side = both_halves.reshape(both_halves.shape[0], root_rows)
    root_update = assembled - transposed_product(panel_side, root_panel)
    return (child_panel[None], root_panel[:, None, None, :], root_update[:, None, None, :])


def solution(mesh):
    return jax.shard_map(
        body,
        mesh=mesh,
        in_specs=(P("half", "row", "col"), P("half", None), P("row", "col", "half", None)),
        out_specs=(
            P("half", None, "col"),
            P(None, "col", "half", None),
            P("row", "col", "half", None),
        ),
        check_vma=False,
    )
```

profile of v0, /device:TPU:1, one launch (start us, length us, event | category | flops | bytes accessed | tf_op | source)
XLA Modules:
  0.0 843.8 jit_solution(4435899986150828886)
XLA Ops:
  7.2 1.3 slice.194
  10.4 1.5 slice.132
  12.8 208.7 %all-gather.14.cloned.1.call-done = f32[8192,32]{1,0:T(8,128)} async-done(((f32[32,32]{1,0:T(8,128)}), f32[8192,32]{1,0:T(8,128)}) %all-gather.14.cloned.1.call-update) | async-done | bytes 1048592 | tf_op jit(solution)/shard_map/all_gather | solution.py:49
  221.5 5.6 copy.23
  227.1 3.5 reshape.68
  232.2 11.7 %cholesky.286 = f32[128,128]{1,0:T(8,128)S(1)} custom-call(f32[128,128]{1,0:T(8,128)S(1)} %cholesky.426), custom_call_target="Cholesky" | custom-call | tf_op jit(solution)/shard_map/jit(cholesky)/cholesky | solution.py:57
  244.0 9.8 %custom-call.31 = f32[1,128,128]{1,2,0:T(8,128)S(1)} custom-call(f32[1,128,128]{2,1,0:T(8,128)S(1)} %get-tuple-element.79), custom_call_target="InvertDiagBlocksLowerTriangular" | custom-call | tf_op jit(solution)/shard_map/jit(cholesky)/cholesky | solution.py:57
  253.9 1.2 constant_dynamic-update-slice_fusion.4
  255.2 1.3 convolution_subtract_fusion.9
  256.4 11.7 %cholesky.305 = f32[128,128]{1,0:T(8,128)S(1)} custom-call(f32[128,128]{1,0:T(8,128)S(1)} %cholesky.430), custom_call_target="Cholesky" | custom-call | tf_op jit(solution)/shard_map/jit(cholesky)/cholesky | solution.py:57
  268.2 10.1 %custom-call.32 = f32[1,128,128]{1,2,0:T(8,128)S(1)} custom-call(f32[1,128,128]{2,1,0:T(8,128)S(1)} %get-tuple-element.76), custom_call_target="InvertDiagBlocksLowerTriangular" | custom-call | tf_op jit(solution)/shard_map/jit(cholesky)/cholesky | solution.py:57
  278.6 1.3 convolution_subtract_fusion.13
  279.9 11.7 %cholesky.326 = f32[128,128]{1,0:T(8,128)S(1)} custom-call(f32[128,128]{1,0:T(8,128)S(1)} %cholesky.435), custom_call_target="Cholesky" | custom-call | tf_op jit(solution)/shard_map/jit(cholesky)/cholesky | solution.py:57
  292.4 9.8 %custom-call.33 = f32[1,128,128]{1,2,0:T(8,128)S(1)} custom-call(f32[1,128,128]{2,1,0:T(8,128)S(1)} %get-tuple-element.73), custom_call_target="InvertDiagBlocksLowerTriangular" | custom-call | tf_op jit(solution)/shard_map/jit(cholesky)/cholesky | solution.py:57
  302.4 1.2 convolution_subtract_fusion.16
  303.6 11.7 %cholesky.343 = f32[128,128]{1,0:T(8,128)S(1)} custom-call(f32[128,128]{1,0:T(8,128)S(1)} %convolution_subtract_fusion.16), custom_call_target="Cholesky" | custom-call | tf_op jit(solution)/shard_map/jit(cholesky)/cholesky | solution.py:57
  319.6 8.5 %while.6 = (s32[]{:T(128)}, f32[512,512]{1,0:T(8,128)S(1)}, s32[4,2]{0,1:T(2,128)S(1)}, f32[4,128,128]{2,1,0:T(8,128)S(1)}, s32[]{:T(128)}) while((s32[]{:T(128)}, f32[512,512]{1,0:T(8,128)S(1)}, s32[4,2]{0,1:T(2,128)S(1)}, f32[4,128,128]{2,1,0:T(8,128)S(1)}, s32[]{:T(128)}) %tuple.64), condition=%wide.while_cond, body=%wide.while_body.sunk | while | flops 2 | bytes 131181 | solution.py:16
  320.3 1.4 bitcast_dynamic-update-slice_fusion.5
  322.4 1.4 bitcast_dynamic-update-slice_fusion.5
  324.5 1.4 bitcast_dynamic-update-slice_fusion.5
  326.6 1.4 bitcast_dynamic-update-slice_fusion.5
  328.1 39.3 %custom-call.34 = f32[4,128,128]{1,2,0:T(8,128)S(1)} custom-call(f32[4,128,128]{2,1,0:T(8,128)S(1)} %get-tuple-element.27), custom_call_target="InvertDiagBlocksLowerTriangular" | custom-call | tf_op jit(solution)/shard_map/triangular_solve/custom-call.3 | solution.py:16
  367.4 1.4 fusion.36
  368.8 1.3 convolution_subtract_fusion.3
  370.5 1.4 convolution_subtract_fusion.2
  373.1 1.6 convolution_subtract_fusion.6
  374.6 1.1 fusion.81
  375.8 1.4 fusion.38
  377.2 1.3 convolution_subtract_fusion.5
  379.0 1.4 convolution_subtract_fusion.4
  380.8 1.6 convolution_subtract_fusion.7
  383.5 3.1 convolution_subtract_fusion
  387.0 1.7 fusion.11
  388.7 1.2 convolution_bitcast_fusion
  390.8 1.1 copy.28
  391.9 23.3 %reduce-scatter.2.cloned.1.call-done = f32[512,1,256]{2,0,1:T(8,128)} async-done(((f32[512,2,256]{2,0,1:T(8,128)}), f32[512,1,256]{2,0,1:T(8,128)}) %reduce-scatter.2.cloned.1.call-update) | async-done | bytes 524304 | tf_op jit(solution)/shard_map/reduce_scatter | solution.py:72
  415.2 1.1 bitcast_add_fusion.2
  417.1 25.4 %all_gather.21 = f32[512,256]{1,0:T(8,128)S(1)} all-gather(f32[32,256]{1,0:T(8,128)S(1)} %slice.211), channel_id=1, replica_groups=mesh['half'=2,'row'=16,'col'=16] {'row'}, dimensions={0}, use_global_device_ids=true | all-gather | bytes 557056 | tf_op jit(solution)/shard_map/all_gather | solution.py:74
  443.3 44.3 %all-reduce.6.cloned.1.call-done = f32[512,32]{0,1:T(8,128)} async-done(((f32[512,32]{0,1:T(8,128)}), f32[512,32]{0,1:T(8,128)}) %all-reduce.6.cloned.1.call-update) | async-done | bytes 65552 | tf_op jit(solution)/shard_map/psum | solution.py:12
  488.1 59.3 %all-gather.10.cloned.1.call-done = f32[512,512]{0,1:T(8,128)} async-done(((f32[512,32]{0,1:T(8,128)}), f32[512,512]{0,1:T(8,128)}) %all-gather.10.cloned.1.call-update) | async-done | bytes 1048592 | tf_op jit(solution)/shard_map/all_gather | solution.py:76
  547.4 1.6 copy.30
  549.0 1.4 fusion.8
  550.5 11.7 %cholesky.358 = f32[128,128]{1,0:T(8,128)S(1)} custom-call(f32[128,128]{1,0:T(8,128)S(1)} %cholesky.439), custom_call_target="Cholesky" | custom-call | tf_op jit(solution)/shard_map/jit(cholesky)/cholesky | solution.py:77
  562.3 9.8 %custom-call.36 = f32[1,128,128]{1,2,0:T(8,128)S(1)} custom-call(f32[1,128,128]{2,1,0:T(8,128)S(1)} %get-tuple-element.69), custom_call_target="InvertDiagBlocksLowerTriangular" | custom-call | tf_op jit(solution)/shard_map/jit(cholesky)/cholesky | solution.py:77
  573.5 11.7 %cholesky.377 = f32[128,128]{1,0:T(8,128)S(1)} custom-call(f32[128,128]{1,0:T(8,128)S(1)} %cholesky.443), custom_call_target="Cholesky" | custom-call | tf_op jit(solution)/shard_map/jit(cholesky)/cholesky | solution.py:77
  586.6 10.0 %custom-call.37 = f32[1,128,128]{1,2,0:T(8,128)S(1)} custom-call(f32[1,128,128]{2,1,0:T(8,128)S(1)} %get-tuple-element.66), custom_call_target="InvertDiagBlocksLowerTriangular" | custom-call | tf_op jit(solution)/shard_map/jit(cholesky)/cholesky | solution.py:77
  596.6 1.2 convolution_dynamic-update-slice_fusion
  598.7 13.2 %cholesky.398 = f32[128,128]{1,0:T(8,128)} custom-call(f32[128,128]{1,0:T(8,128)} %cholesky.448), custom_call_target="Cholesky" | custom-call | tf_op jit(solution)/shard_map/jit(cholesky)/cholesky | solution.py:77
  611.9 1.5 select_reduce_fusion.1
  614.1 11.3 %custom-call.38 = f32[1,128,128]{1,2,0:T(8,128)} custom-call(f32[1,128,128]{2,1,0:T(8,128)} %get-tuple-element.63), custom_call_target="InvertDiagBlocksLowerTriangular" | custom-call | tf_op jit(solution)/shard_map/jit(cholesky)/cholesky | solution.py:77
  626.8 11.7 %cholesky.415 = f32[128,128]{1,0:T(8,128)S(1)} custom-call(f32[128,128]{1,0:T(8,128)S(1)} %convolution_subtract_fusion.15), custom_call_target="Cholesky" | custom-call | tf_op jit(solution)/shard_map/jit(cholesky)/cholesky | solution.py:77
  642.1 8.0 while.5
  642.7 1.4 bitcast_dynamic-update-slice_fusion.4
  644.7 1.4 bitcast_dynamic-update-slice_fusion.4
  646.7 1.4 bitcast_dynamic-update-slice_fusion.4
  648.7 1.4 bitcast_dynamic-update-slice_fusion.4
  650.1 39.3 %custom-call.26 = f32[4,128,128]{1,2,0:T(8,128)S(1)} custom-call(f32[4,128,128]{2,1,0:T(8,128)S(1)} %get-tuple-element.20), custom_call_target="InvertDiagBlocksLowerTriangular" | custom-call | tf_op jit(solution)/shard_map/triangular_solve | solution.py:16
  691.3 1.2 fusion.63
  693.5 115.5 %all-reduce.8.cloned.1.call-done = f32[512,1,256]{2,0,1:T(8,128)} async-done(((f32[512,1,256]{2,0,1:T(8,128)}), f32[512,1,256]{2,0,1:T(8,128)}) %all-reduce.8.cloned.1.call-update) | async-done | bytes 524304 | tf_op jit(solution)/shard_map/psum | solution.py:12
  809.0 2.0 fusion.23
  811.0 1.3 copy.32
  812.3 20.5 %all-gather.12.cloned.1.call-done = f32[512,2,256]{2,0,1:T(8,128)} async-done(((f32[512,1,256]{2,0,1:T(8,128)}), f32[512,2,256]{2,0,1:T(8,128)}) %all-gather.12.cloned.1.call-update) | async-done | bytes 1048592 | tf_op jit(solution)/shard_map/all_gather | solution.py:80
  832.8 1.6 copy.31
  835.4 1.3 copy.33
  (114 shorter events, 30.2 us)
Async XLA Ops:
  7.2 214.4 %all-gather.14.cloned.1.call-start = ((), (), s32[]{:S(2)}) async-start(), calls=%async_computation.7 | async-start | bytes 4210688 | tf_op jit(solution)/shard_map/all_gather | solution.py:49
  8.6 358.8 %all-gather.8.cloned.1.call-start = ((), (), s32[]{:S(2)}) async-start(), calls=%async_computation.1 | async-start | bytes 1114112 | tf_op jit(solution)/shard_map/all_gather | solution.py:59
  10.3 365.4 %all-gather.16.cloned.1.call-start = ((), (), s32[]{:S(2)}) async-start(), calls=%async_computation.8 | async-start | bytes 1114112 | tf_op jit(solution)/shard_map/all_gather | solution.py:48
  11.9 403.3 %reduce-scatter.2.cloned.1.call-start = ((), (), s32[]{:S(2)}) async-start(), calls=%async_computation.2 | async-start | bytes 1572864 | tf_op jit(solution)/shard_map/reduce_scatter | solution.py:72
  231.2 1.0 copy-start
  372.4 0.7 copy-start.3
  375.8 7.7 copy-start.4
  375.8 7.7 copy-start.9
  382.8 0.7 copy-start.5
  388.7 26.5 %copy-start.7 = (f32[512,1,1,256]{3,2,1,0:T(1,128)S(1)}, f32[512,1,1,256]{3,2,1,0:T(1,128)}, u32[]{:S(2)}) copy-start(f32[512,1,1,256]{3,2,1,0:T(1,128)} %param.8) | copy-start | bytes 1572868
  391.9 95.8 %all-reduce.6.cloned.1.call-start = ((), (), s32[]{:S(2)}) async-start(), calls=%async_computation.3 | async-start | bytes 131072 | tf_op jit(solution)/shard_map/psum | solution.py:12
  416.3 0.8 copy-start.1
  443.3 104.1 %all-gather.10.cloned.1.call-start = ((), (), s32[]{:S(2)}) async-start(), calls=%async_computation.4 | async-start | bytes 1114112 | tf_op jit(solution)/shard_map/all_gather | solution.py:76
  487.6 321.3 %all-reduce.8.cloned.1.call-start = ((), (), s32[]{:S(2)}) async-start(), calls=%async_computation.5 | async-start | bytes 1048576 | tf_op jit(solution)/shard_map/psum | solution.py:12
  572.8 0.7 copy-start.6
  689.4 1.5 copy-start.8
  691.3 143.1 %copy-start.2 = (f32[512,256]{1,0:T(8,128)S(1)}, f32[512,256]{1,0:T(8,128)}, u32[]{:S(2)}) copy-start(f32[512,256]{1,0:T(8,128)} %copy-done.1) | copy-start | bytes 1572868
  693.5 139.4 %all-gather.12.cloned.1.call-start = ((), (), s32[]{:S(2)}) async-start(), calls=%async_computation.6 | async-start | bytes 1572864 | tf_op jit(solution)/shard_map/all_gather | solution.py:80
Sparse Core Ops, SparseCore 0:
  13.1 208.4 all-gather.13
  225.1 59.3 all-gather.7
  287.2 63.0 all-gather.15
  392.0 23.1 reduce-scatter.1
  443.4 44.1 all-reduce.5
  490.9 56.4 all-gather.9
  693.6 115.3 all-reduce.7
  811.1 21.7 all-gather.11
where the time goes:
time: 855 us; the launch traced here: 844 us
  waiting for transfers between devices  472 us (55%)
  other arithmetic  249 us (29%)
  local copies, waits for them, and re-layouts  43.5 us (5%)
  matrix products  33.7 us (4%)
  blocking collectives  25.4 us (3%)
  between operations  20.1 us (2%)
    all_gather x1, waiting for transfers between devices, body(): lax.all_gather(child_block[None, :pivot_count, :pivot_count], ('row', 'co...  209 us
    psum x2, waiting for transfers between devices, spread_2(): return lax.psum(kept, axis)  160 us
    another operation x15, other arithmetic, body(): root_factor = jnp.linalg.cholesky(root_corner)  83.6 us
    another operation x5, other arithmetic, lower_solve(): lax.linalg.triangular_solve(factor, right, left_side=True, lower=True)  79.1 us
    another operation x14, other arithmetic, body(): factor = jnp.linalg.cholesky(corner)  78.8 us
    all_gather x1, waiting for transfers between devices, body(): root_corner = lax.all_gather(pivots, 'col', axis=1, tiled=True)  59.3 us
    all_gather x1, blocking collectives, body(): lax.all_gather(assembled[:pivot_count, :], 'row', axis=0, tiled=True)  25.4 us
    reduce_scatter x1, waiting for transfers between devices, body(): lax.psum_scatter(additions, 'half', scatter_dimension=1, tiled=True)  23.3 us
  transfers between devices with their start and end apart: 8, of which 6 were waited for; matrix products, arithmetic and copies ran while one was open for 19% of the time, Pallas kernels for 0%

commit v1 on v0

v1 whole, which is shorter than its diff:
```python
import functools

import jax
import jax.numpy as jnp
from jax import lax
from jax.experimental import pallas as pl
from jax.experimental.pallas import tpu as pltpu
from jax.sharding import PartitionSpec as P

N = 16
PB = 32
BLK = 128
ORD = N * PB
F32 = jnp.float32
MESH = pl.DeviceIdType.MESH
VM = pl.BlockSpec(memory_space=pltpu.VMEM)
SM = pl.BlockSpec(memory_space=pltpu.SMEM)


def dot(a, b):
    return lax.dot_general(
        a, b, (((1,), (0,)), ((), ())), precision=lax.Precision.HIGHEST, preferred_element_type=F32
    )


def dot_t(a, b):
    return lax.dot_general(
        a, b, (((0,), (0,)), ((), ())), precision=lax.Precision.HIGHEST, preferred_element_type=F32
    )


def factor_tile(a, at_half):
    n, full = BLK // 8, (8, BLK)
    lane = lax.broadcasted_iota(jnp.int32, full, 1)
    sub = lax.broadcasted_iota(jnp.int32, full, 0)
    rows = [a[8 * i : 8 * i + 8] for i in range(n)]
    inv = [jnp.where(lane == sub + 8 * i, 1.0, 0.0).astype(F32) for i in range(n)]
    out = []
    for m in range(n):
        if m == n // 2:
            at_half()
        j0 = 8 * m
        top, eye = rows[m], inv[m]
        cols = [jnp.broadcast_to(top[:, j0 + k : j0 + k + 1], full) for k in range(8)]
        e = {(i, k): jnp.broadcast_to(cols[k][i : i + 1], full) for k in range(8) for i in range(k, 8)}
        u = [jnp.broadcast_to(top[i : i + 1], full) for i in range(8)]
        x = [jnp.broadcast_to(eye[i : i + 1], full) for i in range(8)]
        r, low = [None] * 8, {}
        for k in range(8):
            r[k] = lax.rsqrt(e[k, k])
            for i in range(k + 1, 8):
                low[i, k] = e[i, k] * r[k]
            for i in range(k + 1, 8):
                for j in range(k + 1, i + 1):
                    e[i, j] = e[i, j] - low[i, k] * low[j, k]
            u[k] = u[k] * r[k]
            x[k] = x[k] * r[k]
            for i in range(k + 1, 8):
                u[i] = u[i] - low[i, k] * u[k]
                x[i] = x[i] - low[i, k] * x[k]
        done = x[0]
        for k in range(1, 8):
            done = jnp.where(sub == k, x[k], done)
        out.append(done)
        for q in range(m + 1, n):
            src = rows[q]
            t, w, lq = src, inv[q], []
            for k in range(8):
                v = jnp.broadcast_to(src[:, j0 + k : j0 + k + 1], full)
                for p in range(k):
                    v = v - lq[p] * low[k, p]
                v = v * r[k]
                lq.append(v)
                t = t - v * u[k]
                w = w - v * x[k]
            rows[q], inv[q] = t, w
    return jnp.concatenate(out, axis=0)


def factor(a_ref, i_ref, relay):
    def step(j, carry):
        relay(2 * j + 1)
        jb = pl.multiple_of(j * BLK, BLK)
        inv = factor_tile(a_ref[pl.ds(jb, BLK), pl.ds(jb, BLK)], lambda: relay(2 * j + 2))
        i_ref[j] = inv
        a_ref[pl.ds(jb, BLK), :] = dot(inv, a_ref[pl.ds(jb, BLK), :])
        for i in range(1, ORD // BLK):

            @pl.when(i > j)
            def _(i=i):
                here = slice(BLK * i, BLK * i + BLK)
                a_ref[here, :] -= dot_t(a_ref[pl.ds(jb, BLK), here], a_ref[pl.ds(jb, BLK), :])

        return carry

    lax.fori_loop(0, ORD // BLK, step, 0)


def solve(a_ref, i_ref, s_ref, y_ref):
    for j in range(ORD // BLK):
        here = slice(BLK * j, BLK * j + BLK)
        acc = s_ref[here, :]
        if j:
            acc = acc - dot_t(a_ref[0 : BLK * j, here], y_ref[0 : BLK * j, :])
        y_ref[here, :] = dot(i_ref[j], acc)


def remote(src, dst, sends, recvs, k, dev):
    return pltpu.make_async_remote_copy(
        src_ref=src,
        dst_ref=dst,
        send_sem=sends.at[k],
        recv_sem=recvs.at[k],
        device_id=dev,
        device_id_type=MESH,
    )


def each(lo, hi, fn):
    def go(k, carry):
        fn(k)
        return carry

    lax.fori_loop(lo, hi, go, 0)


def rows_of(k):
    return pl.ds(pl.multiple_of(k * PB, PB), PB)


def ring(ref, row, sems):
    rs, rr, ls, lr = sems
    right, left = lax.rem(row + 1, N), lax.rem(row + N - 1, N)

    def to_right(s):
        view = ref.at[rows_of(lax.rem(row - s + N, N)), :]
        return remote(view, view, rs, rr, s, {"row": right})

    def to_left(s):
        view = ref.at[rows_of(lax.rem(row + s, N)), :]
        return remote(view, view, ls, lr, s, {"row": left})

    def got_right(s):
        view = ref.at[rows_of(lax.rem(row - 1 - s + 2 * N, N)), :]
        return remote(view, view, rs, rr, s, {"row": right})

    def got_left(s):
        view = ref.at[rows_of(lax.rem(row + 1 + s, N)), :]
        return remote(view, view, ls, lr, s, {"row": left})

    def start():
        to_right(0).start()
        to_left(0).start()

    def relay(s):
        @pl.when(s < 8)
        def _():
            got_right(s - 1).wait_recv()
            to_right(s).start()

        @pl.when(s < 7)
        def _():
            got_left(s - 1).wait_recv()
            to_left(s).start()

    def finish():
        got_right(7).wait_recv()
        got_left(6).wait_recv()
        each(0, 8, lambda s: to_right(s).wait_send())
        each(0, 7, lambda s: to_left(s).wait_send())

    return start, relay, finish


def packed_piece(tile):
    turned = jnp.transpose(tile)
    lane = lax.broadcasted_iota(jnp.int32, (8, BLK), 1)
    out = turned[0:8]
    for g in range(1, 4):
        out = jnp.where(lane >= PB * g, pltpu.roll(turned[8 * g : 8 * g + 8], PB * g, 1), out)
    return out


def unpack_pieces(pc_ref, rb_ref):
    lane = lax.broadcasted_iota(jnp.int32, (8, BLK), 1)
    for l in range(4):
        pcs = [pc_ref[4 * l + kk] for kk in range(4)]
        for g in range(4):
            out = None
            for kk in range(4):
                shift = (PB * (kk - g)) % BLK
                v = pltpu.roll(pcs[kk], shift, 1) if shift else pcs[kk]
                out = v if kk == 0 else jnp.where(lane >= PB * kk, v, out)
            rb_ref[8 * g : 8 * g + 8, BLK * l : BLK * l + BLK] = out


def greet(devices):
    barrier = pltpu.get_barrier_semaphore()
    total = 0
    for count, dev in devices:
        each(1, count + 1, lambda k, dev=dev: pl.semaphore_signal(barrier, inc=1, device_id=dev(k), device_id_type=MESH))
        total += count
    pl.semaphore_wait(barrier, total)


def child_kernel(
    map_ref, blk_ref, root_ref, panel_ref, asm_ref,
    pc, rb, a_ref, inv_ref, sc, sr, yr, upd, give, take,
    s1, r1, s2, r2, s3, r3, rs, rr, ls, lr, xs, xr,
):
    half, row, col = lax.axis_index("half"), lax.axis_index("row"), lax.axis_index("col")

    def row_peer(k):
        return {"row": lax.rem(row + k, N)}

    def col_peer(k):
        return {"col": lax.rem(col + k, N)}

    other = {"half": 1 - half}
    piece = packed_piece(blk_ref[0:BLK, 0:BLK])
    pc[row] = piece
    greet([(N - 1, row_peer), (N - 1, col_peer), (1, lambda k: other)])

    def piece_to(k):
        return remote(pc.at[row], pc.at[row], s1, r1, k, row_peer(k))

    def piece_from(k):
        view = pc.at[lax.rem(row - k + N, N)]
        return remote(view, view, s1, r1, k, row_peer(k))

    each(1, N, lambda k: piece_to(k).start())
    sc[rows_of(row), :] = blk_ref[0:PB, :]
    mine = jnp.concatenate([jnp.transpose(blk_ref[BLK * i : BLK * i + BLK, 0:BLK])[0:PB] for i in range(1, 4)], axis=1)
    sr[rows_of(col), :] = mine
    each(1, N, lambda k: piece_from(k).wait_recv())
    unpack_pieces(pc, rb)
    a_ref[rows_of(col), :] = rb[...]

    def block_to(k):
        return remote(rb, a_ref.at[rows_of(col), :], s2, r2, k, col_peer(k))

    def block_from(k):
        return remote(rb, a_ref.at[rows_of(lax.rem(col - k + N, N)), :], s2, r2, k, col_peer(k))

    each(1, N, lambda k: block_to(k).start())
    start, relay, finish = ring(sc, row, (rs, rr, ls, lr))
    start()
    each(1, N, lambda k: block_from(k).wait_recv())

    def column_to(k):
        view = sr.at[rows_of(col), :]
        return remote(view, view, s3, r3, k, col_peer(k))

    def column_from(k):
        view = sr.at[rows_of(lax.rem(col - k + N, N)), :]
        return remote(view, view, s3, r3, k, col_peer(k))

    each(1, N, lambda k: column_to(k).start())
    factor(a_ref, inv_ref, relay)
    finish()
    each(1, N, lambda k: column_from(k).wait_recv())
    solve(a_ref, inv_ref, sc, panel_ref)
    solve(a_ref, inv_ref, sr, yr)
    for u in range(3):
        rows = slice(BLK * u, BLK * u + BLK)
        block = blk_ref[BLK + BLK * u : 2 * BLK + BLK * u, BLK:] - dot_t(yr[:, rows], panel_ref[:, BLK:])
        for v in range(3):
            upd[3 * u + v] = block[:, BLK * v : BLK * v + BLK]

    def source(part, target):
        found = jnp.int32(-1)
        for u in range(3):
            found = jnp.where(map_ref[0, 3 * part + u] == 4 * part + target, jnp.int32(u), found)
        return found

    def tile(p, q):
        value = upd[jnp.maximum(p, 0) * 3 + jnp.maximum(q, 0)]
        return jnp.where(jnp.logical_and(p >= 0, q >= 0), value, 0.0)

    from_rows = [source(row, a) for a in range(4)]
    theirs = [source(col, 2 * (1 - half) + b) for b in range(2)]
    ours = [source(col, 2 * half + b) for b in range(2)]
    for a in range(4):
        for b in range(2):
            give[BLK * a : BLK * a + BLK, BLK * b : BLK * b + BLK] = tile(from_rows[a], theirs[b])
    swap = remote(give, take, xs, xr, 0, other)
    swap.start()
    for a in range(4):
        for b in range(2):
            at = (slice(BLK * a, BLK * a + BLK), slice(BLK * b, BLK * b + BLK))
            asm_ref[at] = root_ref[at] + tile(from_rows[a], ours[b])
    swap.wait_recv()
    asm_ref[...] += take[...]
    swap.wait_send()
    each(1, N, lambda k: piece_to(k).wait_send())
    each(1, N, lambda k: block_to(k).wait_send())
    each(1, N, lambda k: column_to(k).wait_send())


def root_kernel(
    asm_ref, panel_ref, out_ref,
    pc, rb, a_ref, inv_ref, sc, sr, yr,
    s1, r1, s2, r2, s3, r3, s4, r4, rs, rr, ls, lr,
):
    half, row, col = lax.axis_index("half"), lax.axis_index("row"), lax.axis_index("col")
    dma = functools.partial(remote)

    def row_peer(k):
        return {"half": lax.rem(half + k // N, 2), "row": lax.rem(row + lax.rem(k, N), N)}

    def col_peer(k):
        return {"half": lax.rem(half + k // N, 2), "col": lax.rem(col + lax.rem(k, N), N)}

    pc[row] = packed_piece(asm_ref[0:BLK, 0:BLK])
    greet([(2 * N - 1, row_peer), (N - 1, col_peer), (N - 1, lambda k: col_peer(k + N))])

    def piece_to(k):
        return dma(pc.at[row], pc.at[row], s1, r1, k, row_peer(k))

    def piece_from(k):
        view = pc.at[lax.rem(row - lax.rem(k, N) + N, N)]
        return dma(view, view, s1, r1, k, row_peer(k))

    @pl.when(half == 0)
    def _():
        each(1, 2 * N, lambda k: piece_to(k).start())

    sc[rows_of(row), :] = asm_ref[0:PB, :]

    @pl.when(half == 0)
    def _():
        sr[rows_of(col), :] = jnp.concatenate(
            [jnp.transpose(asm_ref[BLK * i : BLK * i + BLK, 0:BLK])[0:PB] for i in range(4)], axis=1
        )
        each(1, N, lambda k: piece_from(k).wait_recv())

    @pl.when(half == 1)
    def _():
        each(N, 2 * N, lambda k: piece_from(k).wait_recv())

    unpack_pieces(pc, rb)
    a_ref[rows_of(col), :] = rb[...]

    def part(c):
        return pl.ds(pl.multiple_of(c * PB + half * 16, 16), 16)

    def other_part(c):
        return pl.ds(pl.multiple_of(c * PB + (1 - half) * 16, 16), 16)

    own_rows = pl.ds(pl.multiple_of(half * 16, 16), 16)

    def block_to(k):
        return dma(rb.at[own_rows, :], a_ref.at[part(col), :], s2, r2, k, col_peer(k))

    def block_from(k):
        view = a_ref.at[part(lax.rem(col - k + N, N)), :]
        return dma(view, view, s2, r2, k, col_peer(k))

    def pass_on(k):
        view = a_ref.at[part(lax.rem(col - k + N, N)), :]
        return dma(view, view, s4, r4, k, {"half": 1 - half})

    def passed(k):
        view = a_ref.at[other_part(lax.rem(col - k + N, N)), :]
        return dma(view, view, s4, r4, k, {"half": 1 - half})

    each(1, N, lambda k: block_to(k).start())
    start, relay, finish = ring(sc, row, (rs, rr, ls, lr))
    start()

    def forward(k):
        block_from(k).wait_recv()
        pass_on(k).start()

    each(1, N, forward)

    def column_to(k):
        view = sr.at[rows_of(col), :]
        return dma(view, view, s3, r3, k, col_peer(k))

    def column_from(k):
        view = sr.at[rows_of(lax.rem(col - lax.rem(k, N) + N, N)), :]
        return dma(view, view, s3, r3, k, col_peer(k))

    @pl.when(half == 0)
    def _():
        each(1, 2 * N, lambda k: column_to(k).start())

    each(1, N, lambda k: passed(k).wait_recv())
    each(1, N, lambda k: pass_on(k).wait_send())
    factor(a_ref, inv_ref, relay)
    finish()

    @pl.when(half == 0)
    def _():
        each(1, N, lambda k: column_from(k).wait_recv())

    @pl.when(half == 1)
    def _():
        each(N, 2 * N, lambda k: column_from(k).wait_recv())

    solve(a_ref, inv_ref, sc, panel_ref)
    solve(a_ref, inv_ref, sr, yr)
    for i in range(4):
        rows = slice(BLK * i, BLK * i + BLK)
        out_ref[rows, :] = asm_ref[rows, :] - dot_t(yr[:, rows], panel_ref[...])
    each(1, N, lambda k: block_to(k).wait_send())

    @pl.when(half == 0)
    def _():
        each(1, 2 * N, lambda k: piece_to(k).wait_send())
        each(1, 2 * N, lambda k: column_to(k).wait_send())


def sems(*sizes):
    return [pltpu.SemaphoreType.DMA((n,)) for n in sizes]


def body(child_front, child_map, root_front):
    root = root_front.reshape(ORD, ORD // 2)
    sds = jax.ShapeDtypeStruct
    panel, asm = pl.pallas_call(
        child_kernel,
        out_shape=[sds((ORD, ORD), F32), sds((ORD, ORD // 2), F32)],
        in_specs=[SM, VM, VM],
        out_specs=[VM, VM],
        scratch_shapes=[
            pltpu.VMEM((N, 8, BLK), F32),
            pltpu.VMEM((PB, ORD), F32),
            pltpu.VMEM((ORD, ORD), F32),
            pltpu.VMEM((4, BLK, BLK), F32),
            pltpu.VMEM((ORD, ORD), F32),
            pltpu.VMEM((ORD, 3 * BLK), F32),
            pltpu.VMEM((ORD, 3 * BLK), F32),
            pltpu.VMEM((9, BLK, BLK), F32),
            pltpu.VMEM((ORD, ORD // 2), F32),
            pltpu.VMEM((ORD, ORD // 2), F32),
            *sems(N, N, N, N, N, N, 8, 8, 8, 8, 1, 1),
        ],
        compiler_params=pltpu.CompilerParams(
            collective_id=0, has_side_effects=True, vmem_limit_bytes=40 * 2**20
        ),
    )(child_map, child_front[0], root)
    root_panel, root_update = pl.pallas_call(
        root_kernel,
        out_shape=[sds((ORD, ORD // 2), F32), sds((ORD, ORD // 2), F32)],
        in_specs=[VM],
        out_specs=[VM, VM],
        scratch_shapes=[
            pltpu.VMEM((N, 8, BLK), F32),
            pltpu.VMEM((PB, ORD), F32),
            pltpu.VMEM((ORD, ORD), F32),
            pltpu.VMEM((4, BLK, BLK), F32),
            pltpu.VMEM((ORD, ORD // 2), F32),
            pltpu.VMEM((ORD, ORD), F32),
            pltpu.VMEM((ORD, ORD), F32),
            *sems(2 * N, 2 * N, N, N, 2 * N, 2 * N, N, N, 8, 8, 8, 8),
        ],
        compiler_params=pltpu.CompilerParams(
            collective_id=1, has_side_effects=True, vmem_limit_bytes=40 * 2**20
        ),
    )(asm)
    return (panel[None], root_panel[:, None, None, :], root_update[:, None, None, :])


def solution(mesh):
    return jax.shard_map(
        body,
        mesh=mesh,
        in_specs=(P("half", "row", "col"), P("half", None), P("row", "col", "half", None)),
        out_specs=(
            P("half", None, "col"),
            P(None, "col", "half", None),
            P("row", "col", "half", None),
        ),
        check_vma=False,
    )
```

time: 855 us -> 138 us (0.16); the launches traced: 844 us -> 136 us
  waiting for transfers between devices: 472 us -> 0 us
  other arithmetic: 249 us -> 0 us
  Pallas kernels: 0 us -> 130 us
  local copies, waits for them, and re-layouts: 43.5 us -> 5.5 us
  matrix products: 33.7 us -> 0 us
  blocking collectives: 25.4 us -> 0 us
  between operations: 20.1 us -> 0.67 us
    all_gather x5 -> x0, waiting for transfers between devices: 289 us -> none  [the longest x1 209 us: body(): lax.all_gather(child_block[None, :pivot_count, :pivot_count], ('row', 'co...]
    another operation x34 -> x0, other arithmetic: 241 us -> none  [the longest x15 83.6 us: body(): root_factor = jnp.linalg.cholesky(root_corner)]
    psum x2 -> x0, waiting for transfers between devices: 160 us -> none  [spread_2(): return lax.psum(kept, axis)]
    pallas_call x0 -> x2, Pallas kernels: none -> 130 us  [the longest x1 73 us: body(): pl.pallas_call(child_kernel, out_shape=[sds((ORD, ORD), F32), sds((ORD, O...]
    another operation x33 -> x0, matrix products: 26.7 us -> none  [the longest x21 17.6 us: lower_solve(): lax.linalg.triangular_solve(factor, right, left_side=True, lower=True)]
    all_gather x1 -> x0, blocking collectives: 25.4 us -> none  [body(): lax.all_gather(assembled[:pivot_count, :], 'row', axis=0, tiled=True)]
    reduce_scatter x1 -> x0, waiting for transfers between devices: 23.3 us -> none  [body(): lax.psum_scatter(additions, 'half', scatter_dimension=1, tiled=True)]
    another operation x35 -> x0, local copies, waits for them, and re-layouts: 17.4 us -> none  [the longest x15 8.61 us: lower_solve(): lax.linalg.triangular_solve(factor, right, left_side=True, lower=True)]
  transfers between devices with their start and end apart: 8 -> 0, of which waited for: 6 -> 0; matrix products, arithmetic and copies ran while one was open for 19% -> 0% of each run, Pallas kernels for 0% -> 0%
where the time goes in v1:
time: 138 us; the launch traced here: 136 us
  Pallas kernels  130 us (94%)
  local copies, waits for them, and re-layouts  5.5 us (4%)
    pallas_call x1, Pallas kernels, body(): pl.pallas_call(child_kernel, out_shape=[sds((ORD, ORD), F32), sds((ORD, O...  73 us
    pallas_call x1, Pallas kernels, body(): pl.pallas_call(root_kernel, out_shape=[sds((ORD, ORD // 2), F32), sds((OR...  57.3 us
    unnamed x8, local copies, waits for them, and re-layouts  5.5 us

profile of v1, /device:TPU:1, one launch (start us, length us, event | category | flops | bytes accessed | tf_op | source)
XLA Modules:
  0.0 136.4 jit_solution(4772357567029097063)
XLA Ops:
  0.6 0.0 copy-start
  0.6 1.2 copy.10
  1.8 0.0 copy-start.1
  1.8 0.2 copy-done
  2.0 0.5 copy-done.1
  2.5 73.0 %shard_map.58 = (f32[512,512]{1,0:T(8,128)S(1)}, f32[512,256]{1,0:T(8,128)S(1)}) custom-call(s32[1,48]{1,0:T(1,128)S(1)} %copy-done.1, f32[512,512]{1,0:T(8,128)S(1)} %bitcast.8, f32[512,256]{1,0:T(8,128)S(1)} %bitcast.7), custom_call_target="tpu_custom_call" | custom-call | tf_op jit(solution)/shard_map/pallas_call | solution.py:422
  75.5 57.3 %shard_map.59 = (f32[512,256]{1,0:T(8,128)S(1)}, f32[512,256]{1,0:T(8,128)S(1)}) custom-call(f32[512,256]{1,0:T(8,128)S(1)} %get-tuple-element.8.asm_ref), custom_call_target="tpu_custom_call" | custom-call | tf_op jit(solution)/shard_map/pallas_call | solution.py:444
  132.8 1.3 copy.6
  134.1 1.3 copy.7
  135.5 1.0 copy.12
Async XLA Ops:
  0.6 1.4 %copy-start = (f32[1,512,512]{2,1,0:T(8,128)S(1)}, f32[1,512,512]{2,1,0:T(8,128)}, u32[]{:S(2)}) copy-start(f32[1,512,512]{2,1,0:T(8,128)} %param.3) | copy-start | bytes 3145732
  1.8 0.7 copy-start.1

commit v2 on v1

v2 whole, which is shorter than its diff:
```python
import jax
import jax.numpy as jnp
from jax import lax
from jax.experimental import pallas as pl
from jax.experimental.pallas import tpu as pltpu
from jax.sharding import PartitionSpec as P

N = 16
PB = 32
BLK = 128
ORD = N * PB
F32 = jnp.float32
MESH = pl.DeviceIdType.MESH
VM = pl.BlockSpec(memory_space=pltpu.VMEM)
SM = pl.BlockSpec(memory_space=pltpu.SMEM)


def dot(a, b):
    return lax.dot_general(
        a, b, (((1,), (0,)), ((), ())), precision=lax.Precision.HIGHEST, preferred_element_type=F32
    )


def dot_t(a, b):
    return lax.dot_general(
        a, b, (((0,), (0,)), ((), ())), precision=lax.Precision.HIGHEST, preferred_element_type=F32
    )


def factor_tile(a, at_half):
    n, full = BLK // 8, (8, BLK)
    lane = lax.broadcasted_iota(jnp.int32, full, 1)
    sub = lax.broadcasted_iota(jnp.int32, full, 0)
    rows = [a[8 * i : 8 * i + 8] for i in range(n)]
    inv = [jnp.where(lane == sub + 8 * i, 1.0, 0.0).astype(F32) for i in range(n)]
    out = []
    for m in range(n):
        if m == n // 2:
            at_half()
        j0 = 8 * m
        top, eye = rows[m], inv[m]
        cols = [jnp.broadcast_to(top[:, j0 + k : j0 + k + 1], full) for k in range(8)]
        e = {(i, k): jnp.broadcast_to(cols[k][i : i + 1], full) for k in range(8) for i in range(k, 8)}
        u = [jnp.broadcast_to(top[i : i + 1], full) for i in range(8)]
        x = [jnp.broadcast_to(eye[i : i + 1], full) for i in range(8)]
        r, low = [None] * 8, {}
        for k in range(8):
            r[k] = lax.rsqrt(e[k, k])
            for i in range(k + 1, 8):
                low[i, k] = e[i, k] * r[k]
            for i in range(k + 1, 8):
                for j in range(k + 1, i + 1):
                    e[i, j] = e[i, j] - low[i, k] * low[j, k]
            u[k] = u[k] * r[k]
            x[k] = x[k] * r[k]
            for i in range(k + 1, 8):
                u[i] = u[i] - low[i, k] * u[k]
                x[i] = x[i] - low[i, k] * x[k]
        done = x[0]
        for k in range(1, 8):
            done = jnp.where(sub == k, x[k], done)
        out.append(done)
        for q in range(m + 1, n):
            src = rows[q]
            t, w, lq = src, inv[q], []
            for k in range(8):
                v = jnp.broadcast_to(src[:, j0 + k : j0 + k + 1], full)
                for p in range(k):
                    v = v - lq[p] * low[k, p]
                v = v * r[k]
                lq.append(v)
                t = t - v * u[k]
                w = w - v * x[k]
            rows[q], inv[q] = t, w
    return jnp.concatenate(out, axis=0)


def factor(a_ref, i_ref, diagonal, others, between):
    n = ORD // BLK

    def step(j, carry):
        jb = pl.multiple_of(j * BLK, BLK)
        diagonal(j)
        for v in range(1, n):

            @pl.when(j == v)
            def _(v=v):
                if v < n - 1:
                    others(v)
                a_ref[BLK * v : BLK * v + BLK, BLK * v :] -= dot_t(
                    a_ref[0 : BLK * v, BLK * v : BLK * v + BLK], a_ref[0 : BLK * v, BLK * v :]
                )

        between(2 * j)
        i_ref[j] = factor_tile(a_ref[pl.ds(jb, BLK), pl.ds(jb, BLK)], lambda: between(2 * j + 1))
        for v in range(n - 1):

            @pl.when(j == v)
            def _(v=v):
                if v == 0:
                    others(v)
                here = (slice(BLK * v, BLK * v + BLK), slice(BLK * v + BLK, ORD))
                a_ref[here] = dot(i_ref[v], a_ref[here])

        return carry

    lax.fori_loop(0, n, step, 0)


def solve(a_ref, i_ref, pairs):
    for j in range(ORD // BLK):
        here = slice(BLK * j, BLK * j + BLK)
        for s_ref, y_ref in pairs:
            acc = s_ref[here, :]
            if j:
                acc = acc - dot_t(a_ref[0 : BLK * j, here], y_ref[0 : BLK * j, :])
            y_ref[here, :] = dot(i_ref[j], acc)


def remote(src, dst, send_sem, recv_sem, dev):
    return pltpu.make_async_remote_copy(
        src_ref=src,
        dst_ref=dst,
        send_sem=send_sem,
        recv_sem=recv_sem,
        device_id=dev,
        device_id_type=MESH,
    )


def each(lo, hi, fn):
    def go(k, carry):
        fn(k)
        return carry

    lax.fori_loop(lo, hi, go, 0)


def rows_of(k):
    return pl.ds(pl.multiple_of(k * PB, PB), PB)


def ring(ref, row, sems):
    rs, rr, ls, lr = sems
    right, left = lax.rem(row + 1, N), lax.rem(row + N - 1, N)

    def to_right(s):
        view = ref.at[rows_of(lax.rem(row - s + N, N)), :]
        return remote(view, view, rs.at[s], rr.at[s], {"row": right})

    def to_left(s):
        view = ref.at[rows_of(lax.rem(row + s, N)), :]
        return remote(view, view, ls.at[s], lr.at[s], {"row": left})

    def got_right(s):
        view = ref.at[rows_of(lax.rem(row - 1 - s + 2 * N, N)), :]
        return remote(view, view, rs.at[s], rr.at[s], {"row": right})

    def got_left(s):
        view = ref.at[rows_of(lax.rem(row + 1 + s, N)), :]
        return remote(view, view, ls.at[s], lr.at[s], {"row": left})

    def start():
        to_right(0).start()
        to_left(0).start()

    def relay(s):
        @pl.when(s < 8)
        def _():
            got_right(s - 1).wait_recv()
            to_right(s).start()

        @pl.when(s < 7)
        def _():
            got_left(s - 1).wait_recv()
            to_left(s).start()

    def finish():
        got_right(7).wait_recv()
        got_left(6).wait_recv()
        each(0, 8, lambda s: to_right(s).wait_send())
        each(0, 7, lambda s: to_left(s).wait_send())

    return start, relay, finish


def packed_piece(tile):
    turned = jnp.transpose(tile)
    lane = lax.broadcasted_iota(jnp.int32, (8, BLK), 1)
    out = turned[0:8]
    for g in range(1, 4):
        out = jnp.where(lane >= PB * g, pltpu.roll(turned[8 * g : 8 * g + 8], PB * g, 1), out)
    return out


def unpack_pieces(pc_ref, rb_ref):
    lane = lax.broadcasted_iota(jnp.int32, (8, BLK), 1)
    for l in range(4):
        pcs = [pc_ref[4 * l + kk] for kk in range(4)]
        for g in range(4):
            out = None
            for kk in range(4):
                shift = (PB * (kk - g)) % BLK
                v = pltpu.roll(pcs[kk], shift, 1) if shift else pcs[kk]
                out = v if kk == 0 else jnp.where(lane >= PB * kk, v, out)
            rb_ref[8 * g : 8 * g + 8, BLK * l : BLK * l + BLK] = out


def greet(devices):
    barrier = pltpu.get_barrier_semaphore()
    total = 0
    for count, dev in devices:
        each(1, count + 1, lambda k, dev=dev: pl.semaphore_signal(barrier, inc=1, device_id=dev(k), device_id_type=MESH))
        total += count
    pl.semaphore_wait(barrier, total)


def row_gather(pc, row, send, recv):
    def to(k):
        return remote(pc.at[row], pc.at[row], send.at[k], recv.at[row], {"row": lax.rem(row + k, N)})

    def got(k):
        view = pc.at[lax.rem(row + k, N)]
        return remote(view, view, send.at[k], recv.at[lax.rem(row + k, N)], {"row": row})

    def start():
        each(1, N, lambda k: to(k).start())

    def wait():
        each(1, N, lambda k: got(k).wait_recv())

    def finish():
        each(1, N, lambda k: to(k).wait_send())

    return start, wait, finish


def corner_gather(rb, a_ref, col, ds, dr, os, orr):
    group = col // 4

    def peer(k):
        return {"col": lax.rem(col + k, N)}

    def tile_lanes(g):
        return pl.ds(pl.multiple_of(g * BLK, BLK), BLK)

    def diag_to(k):
        return remote(
            rb.at[:, tile_lanes(group)], a_ref.at[rows_of(col), tile_lanes(group)], ds.at[k], dr.at[col], peer(k)
        )

    def rest_to(k, v):
        lanes = slice(BLK * v + BLK, ORD)
        return remote(rb.at[:, lanes], a_ref.at[rows_of(col), lanes], os.at[k], orr.at[col], peer(k))

    def start():
        each(1, N, lambda k: diag_to(k).start())
        for v in range(3):

            @pl.when(group == v)
            def _(v=v):
                each(1, N, lambda k: rest_to(k, v).start())

    def diagonal(j):
        def one(i):
            src = 4 * j + i

            @pl.when(src != col)
            def _():
                view = a_ref.at[rows_of(src), tile_lanes(j)]
                remote(view, view, ds.at[0], dr.at[src], {"col": src}).wait_recv()

        each(0, 4, one)

    def others(v):
        def one(i):
            src = 4 * v + i

            @pl.when(src != col)
            def _():
                view = a_ref.at[rows_of(src), BLK * v + BLK : ORD]
                remote(view, view, os.at[0], orr.at[src], {"col": src}).wait_recv()

        each(0, 4, one)

    def finish():
        each(1, N, lambda k: diag_to(k).wait_send())
        for v in range(3):

            @pl.when(group == v)
            def _(v=v):
                each(1, N, lambda k: rest_to(k, v).wait_send())

    return start, diagonal, others, finish


def column_gather(sr, col, send, recv):
    def to(k):
        view = sr.at[rows_of(col), :]
        return remote(view, view, send.at[k], recv.at[col], {"col": lax.rem(col + k, N)})

    def got(k):
        src = lax.rem(col + k, N)
        view = sr.at[rows_of(src), :]
        return remote(view, view, send.at[k], recv.at[src], {"col": col})

    def start():
        each(1, N, lambda k: to(k).start())

    def wait():
        each(1, N, lambda k: got(k).wait_recv())

    def finish():
        each(1, N, lambda k: to(k).wait_send())

    return start, wait, finish


def kernel(
    map_ref, blk_ref, root_ref, panel_ref, rpanel_ref, out_ref,
    pc, rb, a_ref, inv_ref, sc, sr, yr, upd, give, take, rx, cg, ct,
    pc2, rb2, a2, inv2, sc2, sr2, yr2, asm,
    s1, r1, s2, r2, s3, r3, s4, r4, rs, rr, ls, lr, xs, xr,
    s5, r5, s6, r6, s7, r7, s8, r8, rs2, rr2, ls2, lr2,
):
    half, row, col = lax.axis_index("half"), lax.axis_index("row"), lax.axis_index("col")
    other = {"half": 1 - half}
    piece_start, piece_wait, piece_end = row_gather(pc, row, s1, r1)
    block_start, block_diag, block_rest, block_end = corner_gather(rb, a_ref, col, s2, r2, s3, r3)
    column_start, column_wait, column_end = column_gather(sr, col, s4, r4)
    ring_start, relay, ring_end = ring(sc, row, (rs, rr, ls, lr))
    piece_start2, piece_wait2, piece_end2 = row_gather(pc2, row, s5, r5)
    block_start2, block_diag2, block_rest2, block_end2 = corner_gather(rb2, a2, col, s6, r6, s7, r7)
    column_start2, column_wait2, column_end2 = column_gather(sr2, col, s8, r8)
    ring_start2, relay2, ring_end2 = ring(sc2, row, (rs2, rr2, ls2, lr2))

    pc[row] = packed_piece(blk_ref[0:BLK, 0:BLK])
    sc[rows_of(row), :] = blk_ref[0:PB, :]
    greet(
        [
            (N - 1, lambda k: {"row": lax.rem(row + k, N)}),
            (N - 1, lambda k: {"col": lax.rem(col + k, N)}),
            (1, lambda k: other),
        ]
    )
    piece_start()
    ring_start()
    root_corner = remote(root_ref.at[0:PB, 0:BLK], rx, xs.at[0], xr.at[0], other)
    root_corner.start()
    sr[rows_of(col), :] = jnp.concatenate(
        [jnp.transpose(blk_ref[BLK * i : BLK * i + BLK, 0:BLK])[0:PB] for i in range(1, 4)], axis=1
    )
    piece_wait()
    unpack_pieces(pc, rb)
    block_start()
    a_ref[rows_of(col), :] = rb[...]
    relay(1)

    def between(i):
        @pl.when(i == 2)
        def _():
            column_start()

        relay(i + 2)

    factor(a_ref, inv_ref, block_diag, block_rest, between)
    ring_end()
    column_wait()
    solve(a_ref, inv_ref, [(sc, panel_ref), (sr, yr)])

    def source(part, target):
        found = jnp.int32(-1)
        for u in range(3):
            found = jnp.where(map_ref[0, 3 * part + u] == 4 * part + target, jnp.int32(u), found)
        return found

    from_rows = [source(row, a) for a in range(4)]
    theirs = [source(col, 2 * (1 - half) + b) for b in range(2)]
    ours = [source(col, 2 * half + b) for b in range(2)]
    p, q = from_rows[0], source(col, 0)
    inside = jnp.logical_and(p >= 0, q >= 0)

    def pick(which, get):
        return jnp.where(which == 2, get(2), jnp.where(which == 1, get(1), get(0)))

    def lanes(v):
        return slice(BLK + BLK * v, 2 * BLK + BLK * v)

    corner = pick(p, lambda u: pick(q, lambda v: blk_ref[BLK + BLK * u : BLK + BLK * u + PB, lanes(v)])) - dot_t(
        pick(p, lambda u: yr[:, BLK * u : BLK * u + BLK]), pick(q, lambda v: panel_ref[:, lanes(v)])
    )[0:PB]
    cg[...] = jnp.where(inside, corner, 0.0)
    swap_corner = remote(cg, ct, xs.at[1], xr.at[1], other)
    swap_corner.start()
    root_corner.wait_recv()
    base = jnp.where(half == 0, root_ref[0:PB, 0:BLK], rx[...])
    swap_corner.wait_recv()
    corner = base + (cg[...] + ct[...])
    pc2[row] = packed_piece(jnp.concatenate([corner] * 4, axis=0))
    piece_start2()
    for u in range(3):
        rows = slice(BLK * u, BLK * u + BLK)
        block = blk_ref[BLK + BLK * u : 2 * BLK + BLK * u, BLK:] - dot_t(yr[:, rows], panel_ref[:, BLK:])
        for v in range(3):
            upd[3 * u + v] = block[:, BLK * v : BLK * v + BLK]

    def tile(p, q):
        value = upd[jnp.maximum(p, 0) * 3 + jnp.maximum(q, 0)]
        return jnp.where(jnp.logical_and(p >= 0, q >= 0), value, 0.0)

    for a in range(4):
        for b in range(2):
            give[BLK * a : BLK * a + BLK, BLK * b : BLK * b + BLK] = tile(from_rows[a], theirs[b])
    swap = remote(give, take, xs.at[2], xr.at[2], other)
    swap.start()

    piece_wait2()
    unpack_pieces(pc2, rb2)
    block_start2()
    a2[rows_of(col), :] = rb2[...]
    swap.wait_recv()
    for a in range(4):
        for b in range(2):
            at = (slice(BLK * a, BLK * a + BLK), slice(BLK * b, BLK * b + BLK))
            asm[at] = root_ref[at] + (tile(from_rows[a], ours[b]) + take[at])
    sc2[rows_of(row), :] = asm[0:PB, :]
    ring_start2()
    own_columns = sr2.at[rows_of(col), :]
    copy_columns = remote(own_columns, own_columns, xs.at[3], xr.at[3], other)

    @pl.when(half == 0)
    def _():
        sr2[rows_of(col), :] = jnp.concatenate(
            [jnp.transpose(asm[BLK * i : BLK * i + BLK, 0:BLK])[0:PB] for i in range(4)], axis=1
        )
        copy_columns.start()

    def between2(i):
        @pl.when(i == 2)
        def _():
            @pl.when(half == 1)
            def _():
                copy_columns.wait_recv()

            column_start2()

        @pl.when(i > 0)
        def _():
            relay2(i)

    factor(a2, inv2, block_diag2, block_rest2, between2)
    ring_end2()
    column_wait2()
    solve(a2, inv2, [(sc2, rpanel_ref), (sr2, yr2)])
    for i in range(4):
        rows = slice(BLK * i, BLK * i + BLK)
        out_ref[rows, :] = asm[rows, :] - dot_t(yr2[:, rows], rpanel_ref[...])

    @pl.when(half == 0)
    def _():
        copy_columns.wait_send()

    for copy in (root_corner, swap_corner, swap):
        copy.wait_send()
    for end in (piece_end, block_end, column_end, piece_end2, block_end2, column_end2):
        end()


def body(child_front, child_map, root_front):
    sds = jax.ShapeDtypeStruct
    full, side = (ORD, ORD), (ORD, ORD // 2)
    sems = [N] * 8 + [8] * 4 + [4, 4] + [N] * 8 + [8] * 4
    shapes = [
        (N, 8, BLK), (PB, ORD), full, (4, BLK, BLK), full, (ORD, 3 * BLK), (ORD, 3 * BLK), (9, BLK, BLK), side, side,
        (PB, BLK), (PB, BLK), (PB, BLK), (N, 8, BLK), (PB, ORD), full, (4, BLK, BLK), side, full, full, side,
    ]
    panel, root_panel, root_update = pl.pallas_call(
        kernel,
        out_shape=[sds(full, F32), sds(side, F32), sds(side, F32)],
        in_specs=[SM, VM, VM],
        out_specs=[VM, VM, VM],
        scratch_shapes=[*(pltpu.VMEM(s, F32) for s in shapes), *(pltpu.SemaphoreType.DMA((n,)) for n in sems)],
        compiler_params=pltpu.CompilerParams(
            collective_id=0, has_side_effects=True, vmem_limit_bytes=48 * 2**20
        ),
    )(child_map, child_front[0], root_front.reshape(side))
    return (panel[None], root_panel[:, None, None, :], root_update[:, None, None, :])


def solution(mesh):
    return jax.shard_map(
        body,
        mesh=mesh,
        in_specs=(P("half", "row", "col"), P("half", None), P("row", "col", "half", None)),
        out_specs=(
            P("half", None, "col"),
            P(None, "col", "half", None),
            P("row", "col", "half", None),
        ),
        check_vma=False,
    )
```

time: 138 us -> 118 us (0.86)
  Pallas kernels: 130 us -> 111 us
    pallas_call x2 -> x1, Pallas kernels: 130 us -> 111 us  [body(): pl.pallas_call(kernel, out_shape=[sds(full, F32), sds(side, F32), sds(sid...]
where the time goes in v2:
time: 118 us; the launch traced here: 117 us
  Pallas kernels  111 us (94%)
  local copies, waits for them, and re-layouts  5.5 us (5%)
    pallas_call x1, Pallas kernels, body(): pl.pallas_call(kernel, out_shape=[sds(full, F32), sds(side, F32), sds(sid...  111 us
    unnamed x8, local copies, waits for them, and re-layouts  5.5 us

profile of v2, /device:TPU:1, one launch (start us, length us, event | category | flops | bytes accessed | tf_op | source)
XLA Modules:
  0.0 117.2 jit_solution(5025789817933374743)
XLA Ops:
  0.6 0.0 copy-start
  0.6 1.2 copy.10
  1.8 0.0 copy-start.1
  1.8 0.2 copy-done
  2.0 0.5 copy-done.1
  2.5 111.0 %shard_map.58 = (f32[512,512]{1,0:T(8,128)S(1)}, f32[512,256]{1,0:T(8,128)S(1)}, f32[512,256]{1,0:T(8,128)S(1)}) custom-call(s32[1,48]{1,0:T(1,128)S(1)} %copy-done.1, f32[512,512]{1,0:T(8,128)S(1)} %bitcast.8, f32[512,256]{1,0:T(8,128)S(1)} %bitcast.7), custom_call_target="tpu_custom_call" | custom-call | tf_op jit(solution)/shard_map/pallas_call | solution.py:477
  113.5 1.3 %copy.6 = f32[512,1,1,256]{3,2,1,0:T(1,128)} copy(f32[512,1,1,256]{3,0,2,1:T(8,128)S(1)} %bitcast.11) | data formatting | bytes 1048576
  114.9 1.3 %copy.7 = f32[512,1,1,256]{3,2,1,0:T(1,128)} copy(f32[512,1,1,256]{3,0,2,1:T(8,128)S(1)} %bitcast.10) | data formatting | bytes 1048576
  116.2 1.0 copy.12
Async XLA Ops:
  0.6 1.4 %copy-start = (f32[1,512,512]{2,1,0:T(8,128)S(1)}, f32[1,512,512]{2,1,0:T(8,128)}, u32[]{:S(2)}) copy-start(f32[1,512,512]{2,1,0:T(8,128)} %param.3) | copy-start | bytes 3145732
  1.8 0.7 copy-start.1

commit v3 on v2

--- a/solution.py
+++ b/solution.py
@@ -29,40 +29,47 @@
 
 def factor_tile(a, at_half):
     n, full = BLK // 8, (8, BLK)
+    diag = lax.broadcasted_iota(jnp.int32, (BLK, BLK), 0) == lax.broadcasted_iota(jnp.int32, (BLK, BLK), 1)
+    only = jnp.where(diag, a, 0.0)
+    scale = lax.rsqrt(jnp.sum(only, axis=0, keepdims=True))
+    a = a * lax.rsqrt(jnp.sum(only, axis=1, keepdims=True)) * scale
     lane = lax.broadcasted_iota(jnp.int32, full, 1)
     sub = lax.broadcasted_iota(jnp.int32, full, 0)
     rows = [a[8 * i : 8 * i + 8] for i in range(n)]
-    inv = [jnp.where(lane == sub + 8 * i, 1.0, 0.0).astype(F32) for i in range(n)]
     out = []
     for m in range(n):
         if m == n // 2:
             at_half()
         j0 = 8 * m
-        top, eye = rows[m], inv[m]
-        cols = [jnp.broadcast_to(top[:, j0 + k : j0 + k + 1], full) for k in range(8)]
+        left = lane < j0 + 8
+        pivots = jnp.logical_and(lane >= j0, left)
+        cols = [jnp.broadcast_to(rows[m][:, j0 + k : j0 + k + 1], full) for k in range(8)]
         e = {(i, k): jnp.broadcast_to(cols[k][i : i + 1], full) for k in range(8) for i in range(k, 8)}
+        top = jnp.where(pivots, jnp.where(lane == sub + j0, 1.0, 0.0), rows[m])
         u = [jnp.broadcast_to(top[i : i + 1], full) for i in range(8)]
-        x = [jnp.broadcast_to(eye[i : i + 1], full) for i in range(8)]
         r, low = [None] * 8, {}
-        for k in range(8):
-            r[k] = lax.rsqrt(e[k, k])
+        for k in range(0, 8, 2):
+            pa, pb, pc = e[k, k], e[k + 1, k], e[k + 1, k + 1]
+            r[k] = lax.rsqrt(pa)
+            r[k + 1] = lax.rsqrt(pa * pc - pb * pb) * (pa * r[k])
             for i in range(k + 1, 8):
                 low[i, k] = e[i, k] * r[k]
-            for i in range(k + 1, 8):
-                for j in range(k + 1, i + 1):
-                    e[i, j] = e[i, j] - low[i, k] * low[j, k]
-            u[k] = u[k] * r[k]
-            x[k] = x[k] * r[k]
-            for i in range(k + 1, 8):
-                u[i] = u[i] - low[i, k] * u[k]
-                x[i] = x[i] - low[i, k] * x[k]
-        done = x[0]
+            for i in range(k + 2, 8):
+                low[i, k + 1] = (e[i, k + 1] - low[i, k] * low[k + 1, k]) * r[k + 1]
+            for i in range(k + 2, 8):
+                for j in range(k + 2, i + 1):
+                    e[i, j] = (e[i, j] - low[i, k] * low[j, k]) - low[i, k + 1] * low[j, k + 1]
+            for p in (k, k + 1):
+                u[p] = u[p] * r[p]
+                for i in range(p + 1, 8):
+                    u[i] = u[i] - low[i, p] * u[p]
+        done = u[0]
         for k in range(1, 8):
-            done = jnp.where(sub == k, x[k], done)
-        out.append(done)
+            done = jnp.where(sub == k, u[k], done)
+        out.append(jnp.where(left, done, 0.0))
         for q in range(m + 1, n):
             src = rows[q]
-            t, w, lq = src, inv[q], []
+            t, lq = jnp.where(pivots, 0.0, src), []
             for k in range(8):
                 v = jnp.broadcast_to(src[:, j0 + k : j0 + k + 1], full)
                 for p in range(k):
@@ -70,9 +77,8 @@
                 v = v * r[k]
                 lq.append(v)
                 t = t - v * u[k]
-                w = w - v * x[k]
-            rows[q], inv[q] = t, w
-    return jnp.concatenate(out, axis=0)
+            rows[q] = t
+    return jnp.concatenate(out, axis=0) * scale
 
 
 def factor(a_ref, i_ref, diagonal, others, between):
@@ -142,44 +148,55 @@
 
 def ring(ref, row, sems):
     rs, rr, ls, lr = sems
-    right, left = lax.rem(row + 1, N), lax.rem(row + N - 1, N)
-
-    def to_right(s):
-        view = ref.at[rows_of(lax.rem(row - s + N, N)), :]
-        return remote(view, view, rs.at[s], rr.at[s], {"row": right})
-
-    def to_left(s):
-        view = ref.at[rows_of(lax.rem(row + s, N)), :]
-        return remote(view, view, ls.at[s], lr.at[s], {"row": left})
-
-    def got_right(s):
-        view = ref.at[rows_of(lax.rem(row - 1 - s + 2 * N, N)), :]
-        return remote(view, view, rs.at[s], rr.at[s], {"row": right})
-
-    def got_left(s):
-        view = ref.at[rows_of(lax.rem(row + 1 + s, N)), :]
-        return remote(view, view, ls.at[s], lr.at[s], {"row": left})
+    right, left = {"row": lax.rem(row + 1, N)}, {"row": lax.rem(row + N - 1, N)}
+    wide = ref.shape[1] // 2
+
+    def part(block, p):
+        return ref.at[rows_of(block), wide * p : wide * p + wide]
+
+    def to_right(s, p):
+        view = part(lax.rem(row - s + N, N), p)
+        return remote(view, view, rs.at[2 * s + p], rr.at[2 * s + p], right)
+
+    def to_left(s, p):
+        view = part(lax.rem(row + s, N), p)
+        return remote(view, view, ls.at[2 * s + p], lr.at[2 * s + p], left)
+
+    def got_right(s, p):
+        view = part(lax.rem(row - 1 - s + 2 * N, N), p)
+        return remote(view, view, rs.at[2 * s + p], rr.at[2 * s + p], right)
+
+    def got_left(s, p):
+        view = part(lax.rem(row + 1 + s, N), p)
+        return remote(view, view, ls.at[2 * s + p], lr.at[2 * s + p], left)
 
     def start():
-        to_right(0).start()
-        to_left(0).start()
+        for p in range(2):
+            to_right(0, p).start()
+            to_left(0, p).start()
 
     def relay(s):
-        @pl.when(s < 8)
-        def _():
-            got_right(s - 1).wait_recv()
-            to_right(s).start()
-
         @pl.when(s < 7)
         def _():
-            got_left(s - 1).wait_recv()
-            to_left(s).start()
+            for p in range(2):
+                got_right(s - 1, p).wait_recv()
+                to_right(s, p).start()
+                got_left(s - 1, p).wait_recv()
+                to_left(s, p).start()
+
+        @pl.when(s == 7)
+        def _():
+            for p in range(2):
+                got_right(s - 1, p).wait_recv()
+                to_right(s, p).start()
 
     def finish():
-        got_right(7).wait_recv()
-        got_left(6).wait_recv()
-        each(0, 8, lambda s: to_right(s).wait_send())
-        each(0, 7, lambda s: to_left(s).wait_send())
+        for p in range(2):
+            got_right(7, p).wait_recv()
+            got_left(6, p).wait_recv()
+        for p in range(2):
+            each(0, 8, lambda s, p=p: to_right(s, p).wait_send())
+            each(0, 7, lambda s, p=p: to_left(s, p).wait_send())
 
     return start, relay, finish
 
@@ -208,11 +225,9 @@
 
 def greet(devices):
     barrier = pltpu.get_barrier_semaphore()
-    total = 0
     for count, dev in devices:
         each(1, count + 1, lambda k, dev=dev: pl.semaphore_signal(barrier, inc=1, device_id=dev(k), device_id_type=MESH))
-        total += count
-    pl.semaphore_wait(barrier, total)
+    return lambda: pl.semaphore_wait(barrier, sum(count for count, _ in devices))
 
 
 def row_gather(pc, row, send, recv):
@@ -253,12 +268,11 @@
         lanes = slice(BLK * v + BLK, ORD)
         return remote(rb.at[:, lanes], a_ref.at[rows_of(col), lanes], os.at[k], orr.at[col], peer(k))
 
-    def start():
-        each(1, N, lambda k: diag_to(k).start())
-        for v in range(3):
-
-            @pl.when(group == v)
-            def _(v=v):
+    def start(v):
+        @pl.when(group == v)
+        def _():
+            each(1, N, lambda k: diag_to(k).start())
+            if v < 3:
                 each(1, N, lambda k: rest_to(k, v).start())
 
     def diagonal(j):
@@ -316,10 +330,15 @@
     return start, wait, finish
 
 
+def split_sides(src, dst):
+    for t in range(2):
+        dst[:, BLK * t : BLK * t + BLK] = src[pl.ds(t, ORD, stride=2), :]
+
+
 def kernel(
     map_ref, blk_ref, root_ref, panel_ref, rpanel_ref, out_ref,
     pc, rb, a_ref, inv_ref, sc, sr, yr, upd, give, take, rx, cg, ct,
-    pc2, rb2, a2, inv2, sc2, sr2, yr2, asm,
+    pc2, rb2, a2, inv2, sc2, sr2, yr2, asm, root, rp,
     s1, r1, s2, r2, s3, r3, s4, r4, rs, rr, ls, lr, xs, xr,
     s5, r5, s6, r6, s7, r7, s8, r8, rs2, rr2, ls2, lr2,
 ):
@@ -334,29 +353,38 @@
     column_start2, column_wait2, column_end2 = column_gather(sr2, col, s8, r8)
     ring_start2, relay2, ring_end2 = ring(sc2, row, (rs2, rr2, ls2, lr2))
 
-    pc[row] = packed_piece(blk_ref[0:BLK, 0:BLK])
-    sc[rows_of(row), :] = blk_ref[0:PB, :]
-    greet(
+    wait_all = greet(
         [
             (N - 1, lambda k: {"row": lax.rem(row + k, N)}),
             (N - 1, lambda k: {"col": lax.rem(col + k, N)}),
             (1, lambda k: other),
         ]
     )
-    piece_start()
-    ring_start()
-    root_corner = remote(root_ref.at[0:PB, 0:BLK], rx, xs.at[0], xr.at[0], other)
-    root_corner.start()
+    pc[row] = packed_piece(blk_ref[0:BLK, 0:BLK])
+    sc[rows_of(row), :] = blk_ref[0:PB, :]
     sr[rows_of(col), :] = jnp.concatenate(
         [jnp.transpose(blk_ref[BLK * i : BLK * i + BLK, 0:BLK])[0:PB] for i in range(1, 4)], axis=1
     )
+    split_sides(root_ref, root)
+    wait_all()
+    piece_start()
+    ring_start()
+    root_corner = remote(root.at[0:PB, 0:BLK], rx, xs.at[0], xr.at[0], other)
+    root_corner.start()
     piece_wait()
     unpack_pieces(pc, rb)
-    block_start()
+    block_start(0)
+    block_start(1)
     a_ref[rows_of(col), :] = rb[...]
     relay(1)
 
     def between(i):
+        for v in (2, 3):
+
+            @pl.when(i == v - 2)
+            def _(v=v):
+                block_start(v)
+
         @pl.when(i == 2)
         def _():
             column_start()
@@ -393,7 +421,7 @@
     swap_corner = remote(cg, ct, xs.at[1], xr.at[1], other)
     swap_corner.start()
     root_corner.wait_recv()
-    base = jnp.where(half == 0, root_ref[0:PB, 0:BLK], rx[...])
+    base = jnp.where(half == 0, root[0:PB, 0:BLK], rx[...])
     swap_corner.wait_recv()
     corner = base + (cg[...] + ct[...])
     pc2[row] = packed_piece(jnp.concatenate([corner] * 4, axis=0))
@@ -416,13 +444,14 @@
 
     piece_wait2()
     unpack_pieces(pc2, rb2)
-    block_start2()
+    block_start2(0)
+    block_start2(1)
     a2[rows_of(col), :] = rb2[...]
     swap.wait_recv()
     for a in range(4):
         for b in range(2):
             at = (slice(BLK * a, BLK * a + BLK), slice(BLK * b, BLK * b + BLK))
-            asm[at] = root_ref[at] + (tile(from_rows[a], ours[b]) + take[at])
+            asm[at] = root[at] + (tile(from_rows[a], ours[b]) + take[at])
     sc2[rows_of(row), :] = asm[0:PB, :]
     ring_start2()
     own_columns = sr2.at[rows_of(col), :]
@@ -436,6 +465,12 @@
         copy_columns.start()
 
     def between2(i):
+        for v in (2, 3):
+
+            @pl.when(i == v - 2)
+            def _(v=v):
+                block_start2(v)
+
         @pl.when(i == 2)
         def _():
             @pl.when(half == 1)
@@ -451,10 +486,14 @@
     factor(a2, inv2, block_diag2, block_rest2, between2)
     ring_end2()
     column_wait2()
-    solve(a2, inv2, [(sc2, rpanel_ref), (sr2, yr2)])
+    solve(a2, inv2, [(sc2, rp), (sr2, yr2)])
+    for t in range(2):
+        rpanel_ref[pl.ds(t, ORD, stride=2), :] = rp[:, BLK * t : BLK * t + BLK]
     for i in range(4):
         rows = slice(BLK * i, BLK * i + BLK)
-        out_ref[rows, :] = asm[rows, :] - dot_t(yr2[:, rows], rpanel_ref[...])
+        block = asm[rows, :] - dot_t(yr2[:, rows], rp[...])
+        for t in range(2):
+            out_ref[pl.ds(2 * BLK * i + t, BLK, stride=2), :] = block[:, BLK * t : BLK * t + BLK]
 
     @pl.when(half == 0)
     def _():
@@ -469,22 +508,23 @@
 def body(child_front, child_map, root_front):
     sds = jax.ShapeDtypeStruct
     full, side = (ORD, ORD), (ORD, ORD // 2)
-    sems = [N] * 8 + [8] * 4 + [4, 4] + [N] * 8 + [8] * 4
+    sems = [N] * 12 + [4, 4] + [N] * 12
     shapes = [
         (N, 8, BLK), (PB, ORD), full, (4, BLK, BLK), full, (ORD, 3 * BLK), (ORD, 3 * BLK), (9, BLK, BLK), side, side,
-        (PB, BLK), (PB, BLK), (PB, BLK), (N, 8, BLK), (PB, ORD), full, (4, BLK, BLK), side, full, full, side,
+        (PB, BLK), (PB, BLK), (PB, BLK), (N, 8, BLK), (PB, ORD), full, (4, BLK, BLK), side, full, full, side, side, side,
     ]
     panel, root_panel, root_update = pl.pallas_call(
         kernel,
-        out_shape=[sds(full, F32), sds(side, F32), sds(side, F32)],
+        out_shape=[sds(full, F32), sds((2 * ORD, BLK), F32), sds((2 * ORD, BLK), F32)],
         in_specs=[SM, VM, VM],
         out_specs=[VM, VM, VM],
         scratch_shapes=[*(pltpu.VMEM(s, F32) for s in shapes), *(pltpu.SemaphoreType.DMA((n,)) for n in sems)],
         compiler_params=pltpu.CompilerParams(
             collective_id=0, has_side_effects=True, vmem_limit_bytes=48 * 2**20
         ),
-    )(child_map, child_front[0], root_front.reshape(side))
-    return (panel[None], root_panel[:, None, None, :], root_update[:, None, None, :])
+    )(child_map, child_front[0], root_front.reshape(2 * ORD, BLK))
+    out = (ORD, 1, 1, ORD // 2)
+    return (panel[None], root_panel.reshape(out), root_update.reshape(out))
 
 
 def solution(mesh):

time: 118 us -> 118 us (level)
    unnamed x8 -> x9, local copies, waits for them, and re-layouts: 5.5 us -> 5.47 us
where the time goes in v3:
time: 118 us; the launch traced here: 117 us
  Pallas kernels  111 us (94%)
  local copies, waits for them, and re-layouts  5.47 us (5%)
    pallas_call x1, Pallas kernels, body(): pl.pallas_call(kernel, out_shape=[sds(full, F32), sds((2 * ORD, BLK), F32...  111 us
    unnamed x9, local copies, waits for them, and re-layouts  5.47 us

profile of v3, /device:TPU:1, one launch (start us, length us, event | category | flops | bytes accessed | tf_op | source)
XLA Modules:
  0.0 117.4 jit_solution(443816824978004848)
XLA Ops:
  0.6 0.0 copy-start.2
  0.6 0.6 copy-done.2
  1.3 0.0 copy-start
  1.3 1.2 %copy-done = f32[1,512,512]{2,1,0:T(8,128)S(1)} copy-done((f32[1,512,512]{2,1,0:T(8,128)S(1)}, f32[1,512,512]{2,1,0:T(8,128)}, u32[]{:S(2)}) %copy-start) | copy-done | bytes 1048600
  2.5 0.0 copy-start.1
  2.5 1.0 copy-done.1
  3.6 111.2 %shard_map.58 = (f32[512,512]{1,0:T(8,128)S(1)}, f32[1024,128]{1,0:T(8,128)S(1)}, f32[1024,128]{1,0:T(8,128)S(1)}) custom-call(s32[1,48]{1,0:T(1,128)S(1)} %copy-done.2, f32[512,512]{1,0:T(8,128)S(1)} %bitcast.5, f32[1024,128]{1,0:T(8,128)S(1)} %bitcast.7), custom_call_target="tpu_custom_call" | custom-call | tf_op jit(solution)/shard_map/pallas_call | solution.py:516
  114.8 1.0 copy.11
  115.8 0.8 copy.12
  116.6 0.8 copy.13
Async XLA Ops:
  0.6 0.7 copy-start.2
  1.3 1.2 %copy-start = (f32[1,512,512]{2,1,0:T(8,128)S(1)}, f32[1,512,512]{2,1,0:T(8,128)}, u32[]{:S(2)}) copy-start(f32[1,512,512]{2,1,0:T(8,128)} %param.3) | copy-start | bytes 3145732
  2.5 1.0 copy-start.1

commit v4 on v3

--- a/solution.py
+++ b/solution.py
@@ -81,21 +81,27 @@
     return jnp.concatenate(out, axis=0) * scale
 
 
-def factor(a_ref, i_ref, diagonal, others, between):
+def factor(a_ref, i_ref, arrived, between):
     n = ORD // BLK
+
+    def tiles(v):
+        return slice(BLK * v, BLK * v + BLK)
+
+    def turn(v):
+        for i in range(v + 1, n):
+            arrived(v, i)
+        for i in range(v + 1, n):
+            a_ref[tiles(v), tiles(i)] = jnp.transpose(a_ref[tiles(i), tiles(v)])
 
     def step(j, carry):
         jb = pl.multiple_of(j * BLK, BLK)
-        diagonal(j)
+        arrived(j, j)
         for v in range(1, n):
 
             @pl.when(j == v)
             def _(v=v):
-                if v < n - 1:
-                    others(v)
-                a_ref[BLK * v : BLK * v + BLK, BLK * v :] -= dot_t(
-                    a_ref[0 : BLK * v, BLK * v : BLK * v + BLK], a_ref[0 : BLK * v, BLK * v :]
-                )
+                turn(v)
+                a_ref[tiles(v), BLK * v :] -= dot_t(a_ref[0 : BLK * v, tiles(v)], a_ref[0 : BLK * v, BLK * v :])
 
         between(2 * j)
         i_ref[j] = factor_tile(a_ref[pl.ds(jb, BLK), pl.ds(jb, BLK)], lambda: between(2 * j + 1))
@@ -104,8 +110,8 @@
             @pl.when(j == v)
             def _(v=v):
                 if v == 0:
-                    others(v)
-                here = (slice(BLK * v, BLK * v + BLK), slice(BLK * v + BLK, ORD))
+                    turn(v)
+                here = (tiles(v), slice(BLK * v + BLK, ORD))
                 a_ref[here] = dot(i_ref[v], a_ref[here])
 
         return carry
@@ -250,62 +256,42 @@
     return start, wait, finish
 
 
-def corner_gather(rb, a_ref, col, ds, dr, os, orr):
+def corner_gather(rb, a_ref, col, send, recv):
     group = col // 4
 
-    def peer(k):
-        return {"col": lax.rem(col + k, N)}
-
-    def tile_lanes(g):
-        return pl.ds(pl.multiple_of(g * BLK, BLK), BLK)
-
-    def diag_to(k):
+    def lanes(v):
+        return pl.ds(pl.multiple_of(v * BLK, BLK), BLK)
+
+    def to(k, v):
+        dst = a_ref.at[rows_of(col), lanes(v)]
         return remote(
-            rb.at[:, tile_lanes(group)], a_ref.at[rows_of(col), tile_lanes(group)], ds.at[k], dr.at[col], peer(k)
+            rb.at[:, lanes(v)], dst, send.at[v * N + k], recv.at[v * N + col], {"col": lax.rem(col + k, N)}
         )
 
-    def rest_to(k, v):
-        lanes = slice(BLK * v + BLK, ORD)
-        return remote(rb.at[:, lanes], a_ref.at[rows_of(col), lanes], os.at[k], orr.at[col], peer(k))
-
     def start(v):
-        @pl.when(group == v)
+        @pl.when(group >= v)
         def _():
-            each(1, N, lambda k: diag_to(k).start())
-            if v < 3:
-                each(1, N, lambda k: rest_to(k, v).start())
-
-    def diagonal(j):
+            each(1, N, lambda k: to(k, v).start())
+
+    def arrived(v, g):
         def one(i):
-            src = 4 * j + i
+            src = 4 * g + i
 
             @pl.when(src != col)
             def _():
-                view = a_ref.at[rows_of(src), tile_lanes(j)]
-                remote(view, view, ds.at[0], dr.at[src], {"col": src}).wait_recv()
+                view = a_ref.at[rows_of(src), lanes(v)]
+                remote(view, view, send.at[0], recv.at[v * N + src], {"col": src}).wait_recv()
 
         each(0, 4, one)
 
-    def others(v):
-        def one(i):
-            src = 4 * v + i
-
-            @pl.when(src != col)
-            def _():
-                view = a_ref.at[rows_of(src), BLK * v + BLK : ORD]
-                remote(view, view, os.at[0], orr.at[src], {"col": src}).wait_recv()
-
-        each(0, 4, one)
-
     def finish():
-        each(1, N, lambda k: diag_to(k).wait_send())
-        for v in range(3):
-
-            @pl.when(group == v)
+        for v in range(4):
+
+            @pl.when(group >= v)
             def _(v=v):
-                each(1, N, lambda k: rest_to(k, v).wait_send())
-
-    return start, diagonal, others, finish
+                each(1, N, lambda k: to(k, v).wait_send())
+
+    return start, arrived, finish
 
 
 def column_gather(sr, col, send, recv):
@@ -339,17 +325,17 @@
     map_ref, blk_ref, root_ref, panel_ref, rpanel_ref, out_ref,
     pc, rb, a_ref, inv_ref, sc, sr, yr, upd, give, take, rx, cg, ct,
     pc2, rb2, a2, inv2, sc2, sr2, yr2, asm, root, rp,
-    s1, r1, s2, r2, s3, r3, s4, r4, rs, rr, ls, lr, xs, xr,
-    s5, r5, s6, r6, s7, r7, s8, r8, rs2, rr2, ls2, lr2,
+    s1, r1, s2, r2, s4, r4, rs, rr, ls, lr, xs, xr,
+    s5, r5, s6, r6, s8, r8, rs2, rr2, ls2, lr2,
 ):
     half, row, col = lax.axis_index("half"), lax.axis_index("row"), lax.axis_index("col")
     other = {"half": 1 - half}
     piece_start, piece_wait, piece_end = row_gather(pc, row, s1, r1)
-    block_start, block_diag, block_rest, block_end = corner_gather(rb, a_ref, col, s2, r2, s3, r3)
+    block_start, block_arrived, block_end = corner_gather(rb, a_ref, col, s2, r2)
     column_start, column_wait, column_end = column_gather(sr, col, s4, r4)
     ring_start, relay, ring_end = ring(sc, row, (rs, rr, ls, lr))
     piece_start2, piece_wait2, piece_end2 = row_gather(pc2, row, s5, r5)
-    block_start2, block_diag2, block_rest2, block_end2 = corner_gather(rb2, a2, col, s6, r6, s7, r7)
+    block_start2, block_arrived2, block_end2 = corner_gather(rb2, a2, col, s6, r6)
     column_start2, column_wait2, column_end2 = column_gather(sr2, col, s8, r8)
     ring_start2, relay2, ring_end2 = ring(sc2, row, (rs2, rr2, ls2, lr2))
 
@@ -371,27 +357,28 @@
     ring_start()
     root_corner = remote(root.at[0:PB, 0:BLK], rx, xs.at[0], xr.at[0], other)
     root_corner.start()
+    relay(1)
     piece_wait()
     unpack_pieces(pc, rb)
     block_start(0)
-    block_start(1)
     a_ref[rows_of(col), :] = rb[...]
-    relay(1)
+    relay(2)
+    relay(3)
 
     def between(i):
-        for v in (2, 3):
-
-            @pl.when(i == v - 2)
+        for v in (1, 2, 3):
+
+            @pl.when(i == v - 1)
             def _(v=v):
                 block_start(v)
 
-        @pl.when(i == 2)
+        @pl.when(i == 3)
         def _():
             column_start()
 
-        relay(i + 2)
-
-    factor(a_ref, inv_ref, block_diag, block_rest, between)
+        relay(i + 4)
+
+    factor(a_ref, inv_ref, block_arrived, between)
     ring_end()
     column_wait()
     solve(a_ref, inv_ref, [(sc, panel_ref), (sr, yr)])
@@ -442,11 +429,6 @@
     swap = remote(give, take, xs.at[2], xr.at[2], other)
     swap.start()
 
-    piece_wait2()
-    unpack_pieces(pc2, rb2)
-    block_start2(0)
-    block_start2(1)
-    a2[rows_of(col), :] = rb2[...]
     swap.wait_recv()
     for a in range(4):
         for b in range(2):
@@ -454,6 +436,10 @@
             asm[at] = root[at] + (tile(from_rows[a], ours[b]) + take[at])
     sc2[rows_of(row), :] = asm[0:PB, :]
     ring_start2()
+    piece_wait2()
+    unpack_pieces(pc2, rb2)
+    block_start2(0)
+    a2[rows_of(col), :] = rb2[...]
     own_columns = sr2.at[rows_of(col), :]
     copy_columns = remote(own_columns, own_columns, xs.at[3], xr.at[3], other)
 
@@ -464,14 +450,17 @@
         )
         copy_columns.start()
 
+    relay2(1)
+    relay2(2)
+
     def between2(i):
-        for v in (2, 3):
-
-            @pl.when(i == v - 2)
+        for v in (1, 2, 3):
+
+            @pl.when(i == v - 1)
             def _(v=v):
                 block_start2(v)
 
-        @pl.when(i == 2)
+        @pl.when(i == 3)
         def _():
             @pl.when(half == 1)
             def _():
@@ -479,11 +468,9 @@
 
             column_start2()
 
-        @pl.when(i > 0)
-        def _():
-            relay2(i)
-
-    factor(a2, inv2, block_diag2, block_rest2, between2)
+        relay2(i + 3)
+
+    factor(a2, inv2, block_arrived2, between2)
     ring_end2()
     column_wait2()
     solve(a2, inv2, [(sc2, rp), (sr2, yr2)])
@@ -508,7 +495,7 @@
 def body(child_front, child_map, root_front):
     sds = jax.ShapeDtypeStruct
     full, side = (ORD, ORD), (ORD, ORD // 2)
-    sems = [N] * 12 + [4, 4] + [N] * 12
+    sems = [N, N, 4 * N, 4 * N] + [N] * 6 + [4, 4] + [N, N, 4 * N, 4 * N] + [N] * 6
     shapes = [
         (N, 8, BLK), (PB, ORD), full, (4, BLK, BLK), full, (ORD, 3 * BLK), (ORD, 3 * BLK), (9, BLK, BLK), side, side,
         (PB, BLK), (PB, BLK), (PB, BLK), (N, 8, BLK), (PB, ORD), full, (4, BLK, BLK), side, full, full, side, side, side,

time: 118 us -> 112 us (0.949)
  Pallas kernels: 111 us -> 105 us
    pallas_call x1, Pallas kernels: 111 us -> 105 us  [body(): pl.pallas_call(kernel, out_shape=[sds(full, F32), sds((2 * ORD, BLK), F32...]
where the time goes in v4:
time: 112 us; the launch traced here: 111 us
  Pallas kernels  105 us (94%)
  local copies, waits for them, and re-layouts  5.47 us (5%)
    pallas_call x1, Pallas kernels, body(): pl.pallas_call(kernel, out_shape=[sds(full, F32), sds((2 * ORD, BLK), F32...  105 us
    unnamed x9, local copies, waits for them, and re-layouts  5.47 us

profile of v4, /device:TPU:1, one launch (start us, length us, event | category | flops | bytes accessed | tf_op | source)
XLA Modules:
  0.0 111.1 jit_solution(4923382077845949505)
XLA Ops:
  0.6 0.0 copy-start.2
  0.6 0.6 copy-done.2
  1.3 0.0 copy-start
  1.3 1.2 %copy-done = f32[1,512,512]{2,1,0:T(8,128)S(1)} copy-done((f32[1,512,512]{2,1,0:T(8,128)S(1)}, f32[1,512,512]{2,1,0:T(8,128)}, u32[]{:S(2)}) %copy-start) | copy-done | bytes 1048600
  2.5 0.0 copy-start.1
  2.5 1.0 copy-done.1
  3.6 105.0 %shard_map.58 = (f32[512,512]{1,0:T(8,128)S(1)}, f32[1024,128]{1,0:T(8,128)S(1)}, f32[1024,128]{1,0:T(8,128)S(1)}) custom-call(s32[1,48]{1,0:T(1,128)S(1)} %copy-done.2, f32[512,512]{1,0:T(8,128)S(1)} %bitcast.5, f32[1024,128]{1,0:T(8,128)S(1)} %bitcast.7), custom_call_target="tpu_custom_call" | custom-call | tf_op jit(solution)/shard_map/pallas_call | solution.py:503
  108.6 1.0 copy.11
  109.5 0.8 copy.12
  110.3 0.8 copy.13
Async XLA Ops:
  0.6 0.7 copy-start.2
  1.3 1.2 %copy-start = (f32[1,512,512]{2,1,0:T(8,128)S(1)}, f32[1,512,512]{2,1,0:T(8,128)}, u32[]{:S(2)}) copy-start(f32[1,512,512]{2,1,0:T(8,128)} %param.3) | copy-start | bytes 3145732
  2.5 1.0 copy-start.1

commit v5 on v4

--- a/solution.py
+++ b/solution.py
@@ -324,7 +324,7 @@
 def kernel(
     map_ref, blk_ref, root_ref, panel_ref, rpanel_ref, out_ref,
     pc, rb, a_ref, inv_ref, sc, sr, yr, upd, give, take, rx, cg, ct,
-    pc2, rb2, a2, inv2, sc2, sr2, yr2, asm, root, rp,
+    pc2, rb2, a2, inv2, sc2, sr2, yr2, asm, root, rp, cs, cy,
     s1, r1, s2, r2, s4, r4, rs, rr, ls, lr, xs, xr,
     s5, r5, s6, r6, s8, r8, rs2, rr2, ls2, lr2,
 ):
@@ -372,7 +372,7 @@
             def _(v=v):
                 block_start(v)
 
-        @pl.when(i == 3)
+        @pl.when(i == 2)
         def _():
             column_start()
 
@@ -381,7 +381,6 @@
     factor(a_ref, inv_ref, block_arrived, between)
     ring_end()
     column_wait()
-    solve(a_ref, inv_ref, [(sc, panel_ref), (sr, yr)])
 
     def source(part, target):
         found = jnp.int32(-1)
@@ -401,18 +400,22 @@
     def lanes(v):
         return slice(BLK + BLK * v, 2 * BLK + BLK * v)
 
-    corner = pick(p, lambda u: pick(q, lambda v: blk_ref[BLK + BLK * u : BLK + BLK * u + PB, lanes(v)])) - dot_t(
-        pick(p, lambda u: yr[:, BLK * u : BLK * u + BLK]), pick(q, lambda v: panel_ref[:, lanes(v)])
-    )[0:PB]
+    cs[:, 0:BLK] = pick(q, lambda v: sc[:, lanes(v)])
+    cs[:, BLK:] = pick(p, lambda u: sr[:, BLK * u : BLK * u + BLK])
+    solve(a_ref, inv_ref, [(cs, cy)])
+    corner = pick(p, lambda u: pick(q, lambda v: blk_ref[BLK + BLK * u : BLK + BLK * u + PB, lanes(v)]))
+    corner = corner - dot_t(cy[:, BLK:], cy[:, 0:BLK])[0:PB]
     cg[...] = jnp.where(inside, corner, 0.0)
     swap_corner = remote(cg, ct, xs.at[1], xr.at[1], other)
     swap_corner.start()
+    solve(a_ref, inv_ref, [(sr, yr)])
     root_corner.wait_recv()
     base = jnp.where(half == 0, root[0:PB, 0:BLK], rx[...])
     swap_corner.wait_recv()
     corner = base + (cg[...] + ct[...])
     pc2[row] = packed_piece(jnp.concatenate([corner] * 4, axis=0))
     piece_start2()
+    solve(a_ref, inv_ref, [(sc, panel_ref)])
     for u in range(3):
         rows = slice(BLK * u, BLK * u + BLK)
         block = blk_ref[BLK + BLK * u : 2 * BLK + BLK * u, BLK:] - dot_t(yr[:, rows], panel_ref[:, BLK:])
@@ -429,6 +432,10 @@
     swap = remote(give, take, xs.at[2], xr.at[2], other)
     swap.start()
 
+    piece_wait2()
+    unpack_pieces(pc2, rb2)
+    block_start2(0)
+    a2[rows_of(col), :] = rb2[...]
     swap.wait_recv()
     for a in range(4):
         for b in range(2):
@@ -436,10 +443,6 @@
             asm[at] = root[at] + (tile(from_rows[a], ours[b]) + take[at])
     sc2[rows_of(row), :] = asm[0:PB, :]
     ring_start2()
-    piece_wait2()
-    unpack_pieces(pc2, rb2)
-    block_start2(0)
-    a2[rows_of(col), :] = rb2[...]
     own_columns = sr2.at[rows_of(col), :]
     copy_columns = remote(own_columns, own_columns, xs.at[3], xr.at[3], other)
 
@@ -460,7 +463,7 @@
             def _(v=v):
                 block_start2(v)
 
-        @pl.when(i == 3)
+        @pl.when(i == 2)
         def _():
             @pl.when(half == 1)
             def _():
@@ -499,6 +502,7 @@
     shapes = [
         (N, 8, BLK), (PB, ORD), full, (4, BLK, BLK), full, (ORD, 3 * BLK), (ORD, 3 * BLK), (9, BLK, BLK), side, side,
         (PB, BLK), (PB, BLK), (PB, BLK), (N, 8, BLK), (PB, ORD), full, (4, BLK, BLK), side, full, full, side, side, side,
+        side, side,
     ]
     panel, root_panel, root_update = pl.pallas_call(
         kernel,

time: 112 us -> 118 us (1.054)
  the two profiles are of different devices: /device:TPU:1 before, /device:TPU:6 now
where the time goes in v5:
time: 118 us
  Pallas kernels  112 us (95%)
  local copies, waits for them, and re-layouts  5.47 us (5%)
    pallas_call x1, Pallas kernels, body(): pl.pallas_call(kernel, out_shape=[sds(full, F32), sds((2 * ORD, BLK), F32...  112 us
    unnamed x9, local copies, waits for them, and re-layouts  5.47 us

profile of v5, /device:TPU:6, one launch (start us, length us, event | category | flops | bytes accessed | tf_op | source)
XLA Modules:
  0.0 118.2 jit_solution(7926300786558113284)
XLA Ops:
  0.6 0.0 copy-start.2
  0.6 0.6 copy-done.2
  1.3 0.0 copy-start
  1.3 1.2 %copy-done = f32[1,512,512]{2,1,0:T(8,128)S(1)} copy-done((f32[1,512,512]{2,1,0:T(8,128)S(1)}, f32[1,512,512]{2,1,0:T(8,128)}, u32[]{:S(2)}) %copy-start) | copy-done | bytes 1048600
  2.5 0.0 copy-start.1
  2.5 1.0 copy-done.1
  3.6 112.1 %shard_map.58 = (f32[512,512]{1,0:T(8,128)S(1)}, f32[1024,128]{1,0:T(8,128)S(1)}, f32[1024,128]{1,0:T(8,128)S(1)}) custom-call(s32[1,48]{1,0:T(1,128)S(1)} %copy-done.2, f32[512,512]{1,0:T(8,128)S(1)} %bitcast.5, f32[1024,128]{1,0:T(8,128)S(1)} %bitcast.7), custom_call_target="tpu_custom_call" | custom-call | tf_op jit(solution)/shard_map/pallas_call | solution.py:507
  115.6 1.0 copy.11
  116.6 0.8 copy.12
  117.4 0.8 copy.13
Async XLA Ops:
  0.6 0.7 copy-start.2
  1.3 1.2 %copy-start = (f32[1,512,512]{2,1,0:T(8,128)S(1)}, f32[1,512,512]{2,1,0:T(8,128)}, u32[]{:S(2)}) copy-start(f32[1,512,512]{2,1,0:T(8,128)} %param.3) | copy-start | bytes 3145732
  2.5 1.0 copy-start.1

commit v6 on v4

--- a/solution.py
+++ b/solution.py
@@ -392,27 +392,29 @@
     from_rows = [source(row, a) for a in range(4)]
     theirs = [source(col, 2 * (1 - half) + b) for b in range(2)]
     ours = [source(col, 2 * half + b) for b in range(2)]
-    p, q = from_rows[0], source(col, 0)
-    inside = jnp.logical_and(p >= 0, q >= 0)
+    p = from_rows[0]
 
     def pick(which, get):
         return jnp.where(which == 2, get(2), jnp.where(which == 1, get(1), get(0)))
 
-    def lanes(v):
-        return slice(BLK + BLK * v, 2 * BLK + BLK * v)
-
-    corner = pick(p, lambda u: pick(q, lambda v: blk_ref[BLK + BLK * u : BLK + BLK * u + PB, lanes(v)])) - dot_t(
-        pick(p, lambda u: yr[:, BLK * u : BLK * u + BLK]), pick(q, lambda v: panel_ref[:, lanes(v)])
+    strip = pick(p, lambda u: blk_ref[BLK + BLK * u : BLK + BLK * u + PB, BLK:]) - dot_t(
+        pick(p, lambda u: yr[:, BLK * u : BLK * u + BLK]), panel_ref[:, BLK:]
     )[0:PB]
-    cg[...] = jnp.where(inside, corner, 0.0)
+    for b in range(4):
+        q = source(col, b)
+        part = pick(q, lambda v: strip[:, BLK * v : BLK * v + BLK])
+        cg[:, BLK * b : BLK * b + BLK] = jnp.where(jnp.logical_and(p >= 0, q >= 0), part, 0.0)
     swap_corner = remote(cg, ct, xs.at[1], xr.at[1], other)
     swap_corner.start()
     root_corner.wait_recv()
     base = jnp.where(half == 0, root[0:PB, 0:BLK], rx[...])
     swap_corner.wait_recv()
-    corner = base + (cg[...] + ct[...])
+    corner = base + (cg[:, 0:BLK] + ct[:, 0:BLK])
     pc2[row] = packed_piece(jnp.concatenate([corner] * 4, axis=0))
     piece_start2()
+    joined = cg[...] + ct[...]
+    sc2[rows_of(row), :] = root[0:PB, :] + jnp.where(half == 0, joined[:, 0 : 2 * BLK], joined[:, 2 * BLK :])
+    ring_start2()
     for u in range(3):
         rows = slice(BLK * u, BLK * u + BLK)
         block = blk_ref[BLK + BLK * u : 2 * BLK + BLK * u, BLK:] - dot_t(yr[:, rows], panel_ref[:, BLK:])
@@ -429,13 +431,13 @@
     swap = remote(give, take, xs.at[2], xr.at[2], other)
     swap.start()
 
+    relay2(1)
     swap.wait_recv()
     for a in range(4):
         for b in range(2):
             at = (slice(BLK * a, BLK * a + BLK), slice(BLK * b, BLK * b + BLK))
             asm[at] = root[at] + (tile(from_rows[a], ours[b]) + take[at])
-    sc2[rows_of(row), :] = asm[0:PB, :]
-    ring_start2()
+    relay2(2)
     piece_wait2()
     unpack_pieces(pc2, rb2)
     block_start2(0)
@@ -450,8 +452,7 @@
         )
         copy_columns.start()
 
-    relay2(1)
-    relay2(2)
+    relay2(3)
 
     def between2(i):
         for v in (1, 2, 3):
@@ -460,7 +461,7 @@
             def _(v=v):
                 block_start2(v)
 
-        @pl.when(i == 3)
+        @pl.when(i == 2)
         def _():
             @pl.when(half == 1)
             def _():
@@ -468,7 +469,7 @@
 
             column_start2()
 
-        relay2(i + 3)
+        relay2(i + 4)
 
     factor(a2, inv2, block_arrived2, between2)
     ring_end2()
@@ -498,7 +499,7 @@
     sems = [N, N, 4 * N, 4 * N] + [N] * 6 + [4, 4] + [N, N, 4 * N, 4 * N] + [N] * 6
     shapes = [
         (N, 8, BLK), (PB, ORD), full, (4, BLK, BLK), full, (ORD, 3 * BLK), (ORD, 3 * BLK), (9, BLK, BLK), side, side,
-        (PB, BLK), (PB, BLK), (PB, BLK), (N, 8, BLK), (PB, ORD), full, (4, BLK, BLK), side, full, full, side, side, side,
+        (PB, BLK), (PB, ORD), (PB, ORD), (N, 8, BLK), (PB, ORD), full, (4, BLK, BLK), side, full, full, side, side, side,
     ]
     panel, root_panel, root_update = pl.pallas_call(
         kernel,

time: 112 us -> 112 us (level)
  the two profiles are of different devices: /device:TPU:1 before, /device:TPU:14 now
where the time goes in v6:
time: 112 us; the launch traced here: 111 us
  Pallas kernels  105 us (94%)
  local copies, waits for them, and re-layouts  5.47 us (5%)
    pallas_call x1, Pallas kernels, body(): pl.pallas_call(kernel, out_shape=[sds(full, F32), sds((2 * ORD, BLK), F32...  105 us
    unnamed x9, local copies, waits for them, and re-layouts  5.47 us

profile of v6, /device:TPU:14, one launch (start us, length us, event | category | flops | bytes accessed | tf_op | source)
XLA Modules:
  0.0 111.3 jit_solution(47467357168708962)
XLA Ops:
  0.6 0.0 copy-start.2
  0.6 0.6 copy-done.2
  1.3 0.0 copy-start
  1.3 1.2 %copy-done = f32[1,512,512]{2,1,0:T(8,128)S(1)} copy-done((f32[1,512,512]{2,1,0:T(8,128)S(1)}, f32[1,512,512]{2,1,0:T(8,128)}, u32[]{:S(2)}) %copy-start) | copy-done | bytes 1048600
  2.5 0.0 copy-start.1
  2.5 1.0 copy-done.1
  3.6 105.2 %shard_map.58 = (f32[512,512]{1,0:T(8,128)S(1)}, f32[1024,128]{1,0:T(8,128)S(1)}, f32[1024,128]{1,0:T(8,128)S(1)}) custom-call(s32[1,48]{1,0:T(1,128)S(1)} %copy-done.2, f32[512,512]{1,0:T(8,128)S(1)} %bitcast.5, f32[1024,128]{1,0:T(8,128)S(1)} %bitcast.7), custom_call_target="tpu_custom_call" | custom-call | tf_op jit(solution)/shard_map/pallas_call | solution.py:504
  108.7 1.0 copy.11
  109.7 0.8 copy.12
  110.5 0.8 copy.13
Async XLA Ops:
  0.6 0.7 copy-start.2
  1.3 1.2 %copy-start = (f32[1,512,512]{2,1,0:T(8,128)S(1)}, f32[1,512,512]{2,1,0:T(8,128)}, u32[]{:S(2)}) copy-start(f32[1,512,512]{2,1,0:T(8,128)} %param.3) | copy-start | bytes 3145732
  2.5 1.0 copy-start.1
